TPU v7x, 32 devices: a whole 2x2x4 slice. The times are simulated.
32 devices in a mesh: seq: 8 (over z, y), exp: 4 (over x, core).
Axes of the slice: x: 2, y: 2, z: 4, core: 2. Of those that a mesh axis runs over, the one named last changes fastest.
Arguments:
- qkv_input: bfloat16 [4096, 16, 512], P('seq', 'exp'), may hold values from -6 to 6
- z_gate: bfloat16 [4096, 4096], P('seq', 'exp'), may hold values from -6 to 6
- beta_logit: float32 [4096, 32], P('seq', 'exp'), may hold values from -6 to 6
- decay_input: float32 [4096, 32], P('seq', 'exp'), may hold values from -8 to 8
- decay_rate: float32 [32], P('exp'), may hold values from 1.2207031e-05 to 0.06
- conv_weight: float32 [4, 16, 512], P(None, 'exp'), may hold values from -3 to 3
- cache_state: float32 [8, 32, 128, 128], P('seq', 'exp'), may hold values from -4 to 4
- cache_tail: float32 [8, 3, 16, 512], P('seq', None, 'exp'), may hold values from -6 to 6
- block_request: int32 [64], replicated, may hold values from 0 to 7, never falling along the last dimension, each value on 1 to 32 neighbouring positions
- cache_owner: int32 [8], replicated, may hold values from 0 to 7, each once
- norm_gain: float32 [128], replicated, may hold values from 0.1 to 1.9
- out_weight: bfloat16 [4096, 2048], P('exp'), may hold values from -0.09375 to 0.09375
- residual: bfloat16 [4096, 2048], P(('seq', 'exp')), may hold values from -6 to 6
- post_gain: float32 [2048], replicated, may hold values from 0.1 to 1.9
- expert_ids: int32 [4096, 10], P(('seq', 'exp')), may hold values from 0 to 31, all different within a row; in each aligned block of 128 rows (0 to 127, 128 to 255, ...) at most 48 rows name the same one
- expert_weights: float32 [4096, 10], P(('seq', 'exp')), may hold values from 0.1 to 1
- expert_gate: bfloat16 [32, 2048, 512], P(('seq', 'exp')), may hold values from -0.125 to 0.125
- expert_up: bfloat16 [32, 2048, 512], P(('seq', 'exp')), may hold values from -0.125 to 0.125
- expert_down: bfloat16 [32, 512, 2048], P(('seq', 'exp')), may hold values from -0.25 to 0.25
Outputs:
- layer_out: bfloat16 [4096, 2048], P(('seq', 'exp'))
Inputs may be any that keep to these rules, and one draw needn't show every extreme that they name: Block c belongs to request block_request[c]; requests are numbered in order, each covers 1 to 32 whole blocks, and one covers exactly 32. `cache_owner`: each cache slot belongs to exactly one request. `expert_ids`: the 10 experts of a row differ; in the 128 rows of one device no expert is named more than 48 times, a bound that some block reaches.
All inputs are finite; a program needn't handle non-finite values.
Results may differ from a plain program's by a relative error of at most 0.013.
Values may be sent and summed in bfloat16 or wider, within the bound.
A program may use at most 128 MiB of HBM per device.

v0:
```python
import math

import jax
import jax.numpy as jnp
from jax import lax
from jax.sharding import PartitionSpec as P

D = 2048
HEAD = 128
GROUP = 2
CONV = 4
BLOCK = 64


precise = lax.Precision.HIGHEST


def from_behind(block, axis, distance):
    devices = range(lax.axis_size(axis))
    route = [(i - distance, i) for i in devices if i - distance in devices]
    return lax.ppermute(block, axis, route)


def entering(value, axis, join, neutral):
    place = lax.axis_index(axis)
    gathered = jax.tree.map(
        lambda a, kind: lax.all_gather(a.astype(kind), axis), value, (jnp.bfloat16, jnp.bfloat16)
    )
    state = jax.tree.map(lambda a, e: jnp.zeros_like(a) + jnp.asarray(e, a.dtype), value, neutral)

    def one(step, state):
        return join(
            state,
            jax.tree.map(
                lambda a, own: lax.dynamic_index_in_dim(a, step, 0, False).astype(own.dtype),
                gathered,
                value,
            ),
        )

    return lax.fori_loop(0, place, one, state)


def chain_product(left, right):
    return jnp.einsum("...ik,...kj->...ij", left, right, precision=precise)


def head_split(convolved):
    length = convolved.shape[0]
    group_count = convolved.shape[1]
    query_rows = convolved[..., :HEAD]
    key_rows = convolved[..., HEAD : 2 * HEAD]
    value_rows = convolved[..., 2 * HEAD :].reshape(length, group_count * GROUP, HEAD)
    query_rows = (
        query_rows
        * lax.rsqrt(jnp.sum(query_rows * query_rows, axis=-1, keepdims=True) + 1e-06)
        / math.sqrt(HEAD)
    )
    key_rows = key_rows * lax.rsqrt(jnp.sum(key_rows * key_rows, axis=-1, keepdims=True) + 1e-06)
    query_rows = jnp.repeat(query_rows, GROUP, axis=1)
    key_rows = jnp.repeat(key_rows, GROUP, axis=1)
    return (query_rows, key_rows, value_rows)


def block_parts(query_rows, key_rows, value_rows, beta, log_decay):
    row_width = key_rows.shape[-1]
    span = log_decay.shape[-1]
    running = jnp.cumsum(log_decay, axis=-1)
    later = jnp.arange(span)[:, None]
    earlier = jnp.arange(span)[None, :]
    inclusive = later >= earlier
    spread = running[..., :, None] - running[..., None, :]
    decay_mat = jnp.where(inclusive, jnp.exp(jnp.where(inclusive, spread, 0.0)), 0.0)
    strict_mat = jnp.where(later > earlier, decay_mat, 0.0)
    key_key = jnp.einsum("...id,...jd->...ij", key_rows, key_rows, precision=precise)
    lower_mat = beta[..., :, None] * key_key * strict_mat + jnp.eye(span, dtype=jnp.float32)
    growth = jnp.exp(running)
    right_side = jnp.concatenate(
        [(beta * growth)[..., None] * key_rows, beta[..., None] * value_rows], axis=-1
    )
    solved = lax.linalg.triangular_solve(
        lower_mat, right_side, left_side=True, lower=True, unit_diagonal=True
    )
    weighted_keys = solved[..., :row_width]
    new_values = solved[..., row_width:]
    carried_keys = jnp.exp(running[..., -1:] - running)[..., None] * key_rows
    query_key = (
        jnp.einsum("...id,...jd->...ij", query_rows, key_rows, precision=precise) * decay_mat
    )
    return (growth, weighted_keys, new_values, carried_keys, query_key)


def block_out(parts, query_rows, start_state):
    growth, weighted_keys, new_values, carried_keys, query_key = parts
    fixed_values = new_values - chain_product(weighted_keys, start_state)
    output = growth[..., None] * chain_product(query_rows, start_state)
    output = output + chain_product(query_key, fixed_values)
    return (output, fixed_values)


def gate_norm(core, z_gate, norm_gain):
    scaled = core * lax.rsqrt(jnp.mean(core * core, axis=-1, keepdims=True) + 1e-06) * norm_gain
    return (scaled.reshape(z_gate.shape) * jax.nn.silu(z_gate.astype(jnp.float32))).astype(
        jnp.bfloat16
    )


def combine_maps(earlier_map, later_map):
    return (
        chain_product(later_map[0], earlier_map[0]),
        chain_product(later_map[0], earlier_map[1]) + later_map[1],
    )


def expert_apply(arrived, expert_gate, expert_up, expert_down):
    flat_rows = arrived.reshape(-1, D)
    gate_part = jnp.dot(flat_rows, expert_gate[0], preferred_element_type=jnp.float32)
    up_part = jnp.dot(flat_rows, expert_up[0], preferred_element_type=jnp.float32)
    hidden = (jax.nn.silu(gate_part) * up_part).astype(jnp.bfloat16)
    result = jnp.dot(hidden, expert_down[0], preferred_element_type=jnp.float32).astype(
        jnp.bfloat16
    )
    return result.reshape(arrived.shape)


def local(
    qkv_input,
    z_gate,
    beta_logit,
    decay_input,
    decay_rate,
    conv_weight,
    cache_state,
    cache_tail,
    block_request,
    cache_owner,
    norm_gain,
    out_weight,
    residual,
    post_gain,
    expert_ids,
    expert_weights,
    expert_gate,
    expert_up,
    expert_down,
):
    seq_len, key_heads, row_width = qkv_input.shape
    blocks = seq_len // BLOCK
    head_count = z_gate.shape[1] // HEAD
    seq_count = lax.axis_size("seq")
    exp_count = lax.axis_size("exp")
    previous = jnp.concatenate([jnp.full((1,), -1, jnp.int32), block_request[:-1]])
    starts_all = block_request != previous
    first_block = lax.axis_index("seq") * blocks
    local_request = lax.dynamic_slice_in_dim(block_request, first_block, blocks, 0)
    local_start = lax.dynamic_slice_in_dim(starts_all, first_block, blocks, 0)
    request_ids = jnp.arange(cache_owner.shape[0], dtype=jnp.int32)
    local_slot = jnp.sum(
        jnp.where(local_request[:, None] == request_ids[None, :], cache_owner[None, :], 0), axis=1
    )
    states_all, tails_all = (
        lax.all_gather(cache_state.astype(jnp.bfloat16), "seq", axis=0, tiled=True).astype(
            cache_state.dtype
        ),
        lax.all_gather(cache_tail.astype(jnp.bfloat16), "seq", axis=0, tiled=True).astype(
            cache_tail.dtype
        ),
    )
    cached_tails = tails_all[local_slot]
    rim_rows = from_behind(qkv_input[seq_len - (CONV - 1) :], "seq", 1).astype(jnp.float32)
    inputs = qkv_input.astype(jnp.float32).reshape(blocks, BLOCK, key_heads, row_width)
    before = jnp.concatenate([rim_rows[None], inputs[:-1, BLOCK - (CONV - 1) :]], axis=0)
    before = jnp.where(local_start[:, None, None, None], cached_tails, before)
    extended = jnp.concatenate([before, inputs], axis=1)
    convolved = sum(
        (conv_weight[offset] * extended[:, offset : offset + BLOCK] for offset in range(CONV))
    )
    convolved = jax.nn.silu(convolved).reshape(seq_len, key_heads, row_width)
    query_rows, key_rows, value_rows = head_split(convolved)

    def to_blocks(rows_in):
        return rows_in.reshape(blocks, BLOCK, head_count, HEAD).transpose(0, 2, 1, 3)

    query_blocks = to_blocks(query_rows)
    key_blocks = to_blocks(key_rows)
    value_blocks = to_blocks(value_rows)
    beta = jax.nn.sigmoid(beta_logit).reshape(blocks, BLOCK, head_count).transpose(0, 2, 1)
    log_decay = (
        (-decay_rate[None, :] * jax.nn.softplus(decay_input))
        .reshape(blocks, BLOCK, head_count)
        .transpose(0, 2, 1)
    )
    parts = block_parts(query_blocks, key_blocks, value_blocks, beta, log_decay)
    growth, weighted_keys, new_values, carried_keys, query_key = parts
    eye_mat = jnp.eye(HEAD, dtype=jnp.float32)
    identity = jnp.broadcast_to(eye_mat, (head_count, HEAD, HEAD))
    zero_state = jnp.zeros((head_count, HEAD, HEAD), jnp.float32)

    def compose(carry, item):
        growth_b, weighted_b, values_b, carried_b, is_first, slot = item
        transfer = growth_b[..., -1, None, None] * eye_mat - jnp.einsum(
            "...ik,...ij->...kj", carried_b, weighted_b, precision=precise
        )
        offset_map = jnp.einsum("...ik,...ij->...kj", carried_b, values_b, precision=precise)
        transfer_eff = jnp.where(is_first, 0.0, transfer)
        offset_eff = jnp.where(
            is_first, chain_product(transfer, states_all[slot]) + offset_map, offset_map
        )
        return (combine_maps(carry, (transfer_eff, offset_eff)), None)

    total_map, _ = lax.scan(
        compose,
        (identity, zero_state),
        (growth, weighted_keys, new_values, carried_keys, local_start, local_slot),
    )
    total_transfer, total_offset = total_map
    _, incoming = entering(
        (total_transfer, total_offset), "seq", combine_maps, (identity, zero_state)
    )

    def advance(state, item):
        growth_b, weighted_b, values_b, carried_b, query_key_b, query_b, is_first, slot = item
        start_state = jnp.where(is_first, states_all[slot], state)
        output_b, fixed_values = block_out(
            (growth_b, weighted_b, values_b, carried_b, query_key_b), query_b, start_state
        )
        end_state = growth_b[..., -1, None, None] * start_state + jnp.einsum(
            "...ik,...ij->...kj", carried_b, fixed_values, precision=precise
        )
        return (end_state, output_b)

    _, output = lax.scan(
        advance,
        incoming,
        (
            growth,
            weighted_keys,
            new_values,
            carried_keys,
            query_key,
            query_blocks,
            local_start,
            local_slot,
        ),
    )
    core = output.transpose(0, 2, 1, 3).reshape(seq_len, head_count, HEAD)
    gated = gate_norm(core, z_gate, norm_gain)
    rows_in = gated
    attn = lax.psum_scatter(
        jnp.dot(rows_in, out_weight, preferred_element_type=jnp.float32).astype(jnp.bfloat16),
        "exp",
        scatter_dimension=0,
        tiled=True,
    ).astype(jnp.float32)
    mid_wide = (residual.astype(jnp.float32) + attn).astype(jnp.bfloat16).astype(jnp.float32)
    normed = (
        mid_wide
        * lax.rsqrt(jnp.mean(mid_wide * mid_wide, axis=-1, keepdims=True) + 1e-06)
        * post_gain
    ).astype(jnp.bfloat16)
    route = expert_weights / jnp.sum(expert_weights, axis=-1, keepdims=True)
    token_count, top_count = expert_ids.shape
    expert_count = seq_count * exp_count
    capacity = max(2, token_count * top_count * 6 // (expert_count * 5))
    flat_ids = expert_ids.reshape(-1)
    order_pos = jnp.arange(flat_ids.shape[0], dtype=jnp.int32)
    same_expert = (flat_ids[:, None] == flat_ids[None, :]) & (
        order_pos[None, :] < order_pos[:, None]
    )
    slot_rank = jnp.sum(same_expert, axis=1, dtype=jnp.int32)
    slot_index = flat_ids * capacity + slot_rank
    outgoing = (
        jnp.zeros((expert_count * capacity, D), jnp.bfloat16)
        .at[slot_index]
        .set(normed[order_pos // top_count])
    )
    outgoing = outgoing.reshape(seq_count, exp_count, capacity, D)
    arrived = lax.all_to_all(
        lax.all_to_all(outgoing, "seq", split_axis=0, concat_axis=0, tiled=True),
        "exp",
        split_axis=1,
        concat_axis=1,
        tiled=True,
    )
    results = expert_apply(arrived, expert_gate, expert_up, expert_down)
    returned = lax.all_to_all(
        lax.all_to_all(results, "seq", split_axis=0, concat_axis=0, tiled=True),
        "exp",
        split_axis=1,
        concat_axis=1,
        tiled=True,
    )
    picked = (
        returned.reshape(expert_count * capacity, D)[slot_index]
        .astype(jnp.float32)
        .reshape(token_count, top_count, D)
    )
    moe_sum = jnp.sum(route[..., None] * picked, axis=1)
    return (mid_wide + moe_sum).astype(jnp.bfloat16)


def solution(mesh):
    in_specs = (
        P("seq", "exp", None),
        P("seq", "exp"),
        P("seq", "exp"),
        P("seq", "exp"),
        P("exp"),
        P(None, "exp", None),
        P("seq", "exp", None, None),
        P("seq", None, "exp", None),
        P(),
        P(),
        P(),
        P("exp", None),
        P(("seq", "exp"), None),
        P(),
        P(("seq", "exp"), None),
        P(("seq", "exp"), None),
        P(("seq", "exp"), None, None),
        P(("seq", "exp"), None, None),
        P(("seq", "exp"), None, None),
    )
    out_specs = P(("seq", "exp"), None)
    return jax.shard_map(local, mesh=mesh, in_specs=in_specs, out_specs=out_specs, check_vma=False)
```

profile of v0, /device:TPU:0, one launch (start us, length us, event | category | flops | bytes accessed | tf_op | source)
XLA Modules:
  0.0 1330.6 jit_solution(2075823684228833107)
XLA Ops:
  7.4 4.9 collective-permute-start
  22.5 31.3 %all_gather.18 = bf16[8,3,4,512]{3,2,1,0:T(4,128)(2,1)S(1)} all-gather(bf16[1,3,4,512]{3,2,1,0:T(4,128)(2,1)S(1)} %convert_element_type.86), channel_id=1, replica_groups=mesh['seq'=8,'exp'=4] {'seq'}, dimensions={0}, use_global_device_ids=true | all-gather | bytes 110592 | tf_op jit(solution)/shard_map/all_gather | solution.py:165
  54.7 4.2 convert.6
  59.9 9.0 divide_multiply_fusion
  71.9 2.6 multiply_multiply_fusion
  76.0 4.8 add_bitcast_fusion
  80.9 316.0 %custom-call.3 = f32[8,8,1,64,64]{3,4,2,1,0:T(8,128)} custom-call(f32[8,8,1,64,64]{4,3,2,1,0:T(8,128)} %add_bitcast_fusion), custom_call_target="InvertDiagBlocksLowerTriangular" | custom-call | tf_op jit(solution)/shard_map/triangular_solve | solution.py:81
  396.9 3.1 reshape_reshape.10
  399.9 2.3 bitcast_multiply_fusion.1
  402.2 2.2 bitcast_multiply_fusion.2
  404.5 3.8 fusion.59
  408.3 2.6 fusion.108
  410.9 4.1 convert_element_type.90
  415.8 117.7 %while.39 = (s32[]{:T(128)}, f32[8,128,128]{2,1,0:T(8,128)}, f32[8,128,128]{2,1,0:T(8,128)}, pred[8]{0:T(512)(128)(4,1)S(1)}, f32[8,8,64]{1,2,0:T(8,128)S(1)}, /...) while((s32[]{:T(128)}, f32[8,128,128]{2,1,0:T(8,128)}, ...), condition=%wide.region_4.5_spmd.clone, body=%wide.region_3.4_spmd.clone.sunk | while | flops 806387712 | bytes 11148097 | solution.py:211
  422.5 2.1 fusion.169
  424.5 3.1 fusion.170
  427.7 2.1 fusion.167
  432.5 2.3 fusion.168
  437.3 2.1 fusion.169
  439.4 3.1 fusion.170
  442.5 2.1 fusion.167
  447.3 2.3 fusion.168
  452.1 2.1 fusion.169
  454.2 3.1 fusion.170
  457.4 2.1 fusion.167
  462.1 2.3 fusion.168
  466.9 2.1 fusion.169
  469.0 3.1 fusion.170
  472.2 2.1 fusion.167
  476.9 2.3 fusion.168
  481.7 2.1 fusion.169
  483.8 3.1 fusion.170
  491.8 2.3 fusion.168
  496.5 2.1 fusion.169
  498.6 3.1 fusion.170
  506.6 2.3 fusion.168
  511.4 2.1 fusion.169
  513.5 3.1 fusion.170
  521.4 2.3 fusion.168
  526.2 2.1 fusion.169
  528.3 3.1 fusion.170
  539.9 4.8 fusion.79
  544.7 38.9 %all-gather.8.cloned.1.call-done = bf16[64,128,128]{2,1,0:T(8,128)(2,1)} async-done(((bf16[8,128,128]{2,1,0:T(8,128)(2,1)}), bf16[64,128,128]{2,1,0:T(8,128)(2,1)}) %all-gather.8.cloned.1.call-update) | async-done | bytes 2097168 | tf_op jit(solution)/shard_map/all_gather | solution.py:27
  583.7 49.9 %all-gather.10.cloned.1.call-done = bf16[64,128,128]{2,1,0:T(8,128)(2,1)} async-done(((bf16[8,128,128]{2,1,0:T(8,128)(2,1)}), bf16[64,128,128]{2,1,0:T(8,128)(2,1)}) %all-gather.10.cloned.1.call-update) | async-done | bytes 2097168 | tf_op jit(solution)/shard_map/all_gather | solution.py:27
  633.7 97.9 %while.38 = (s32[]{:T(128)}, f32[8,128,128]{2,1,0:T(8,128)S(1)}, f32[8,8,64,128]{3,2,1,0:T(8,128)}, f32[8,8,64]{1,2,0:T(8,128)S(1)}, pred[8]{0:T(512)(128)(4,1)S...) while((s32[]{:T(128)}, f32[8,128,128]{2,1,0:T(8,128)S(1)}, ...), condition=%wide.region_9.10_spmd, body=%wide.region_8.9_spmd.sunk | while | flops 352911360 | bytes 6567210 | solution.py:232
  731.6 2.2 multiply_reduce_fusion.1
  734.0 2.9 copy.116
  738.1 4.1 convolution_convert_fusion.1
  744.2 38.7 %reduce-scatter.2.cloned.1.call-done = bf16[128,2048]{1,0:T(8,128)(2,1)} async-done(((bf16[512,2048]{1,0:T(8,128)(2,1)}), bf16[128,2048]{1,0:T(8,128)(2,1)}) %reduce-scatter.2.cloned.1.call-update) | async-done | bytes 524304 | tf_op jit(solution)/shard_map/reduce_scatter | solution.py:249
  785.5 34.0 %scatter_custom_fusion = bf16[1536,2048]{1,0:T(8,128)(2,1)} fusion(s32[1280]{0:T(1024)S(1)} %fusion.100, bf16[128,2048]{1,0:T(8,128)(2,1)S(1)} %fusion.89, s32[2048]{0:T(1024)S(1)} %pad_clamp_fusion.1, bf16[]{:T(256)} %constant.108.clone.1), kind=kCustom, calls=%fused_computation.71 | custom fusion | bytes 6291458 | tf_op jit(solution)/shard_map/scatter | solution.py:275
  819.6 143.6 %all_to_all.20 = bf16[8,4,48,2048]{3,2,1,0:T(8,128)(2,1)S(1)} all-to-all(bf16[8,4,48,2048]{3,2,1,0:T(8,128)(2,1)} %bitcast.216), channel_id=1, replica_groups=mesh['seq'=8,'exp'=4] {'seq'}, dimensions={0} | all-to-all | bytes 12582912 | tf_op jit(solution)/shard_map/all_to_all | solution.py:279
  964.3 73.3 %all_to_all.21 = bf16[8,4,48,2048]{3,2,0,1:T(8,128)(2,1)S(1)} all-to-all(bf16[8,4,48,2048]{3,2,0,1:T(8,128)(2,1)S(1)} %copy.122), channel_id=1, replica_groups=mesh['seq'=8,'exp'=4] {'exp'}, dimensions={1} | all-to-all | bytes 12582912 | tf_op jit(solution)/shard_map/all_to_all | solution.py:278
  1038.8 2.6 copy-done.5
  1041.4 5.2 fusion.72
  1046.6 11.7 convolution_convert_fusion
  1058.3 141.7 %all_to_all.22 = bf16[8,4,48,2048]{3,2,1,0:T(8,128)(2,1)S(1)} all-to-all(bf16[8,4,48,2048]{3,2,1,0:T(8,128)(2,1)} %bitcast.225), channel_id=1, replica_groups=mesh['seq'=8,'exp'=4] {'seq'}, dimensions={0} | all-to-all | bytes 12582912 | tf_op jit(solution)/shard_map/all_to_all | solution.py:287
  1200.0 3.2 copy.124
  1203.3 5.6 all-to-all-start.3
  1209.1 70.5 %all-to-all-done.3 = bf16[8,4,48,2048]{3,2,0,1:T(8,128)(2,1)} async-done(((bf16[8,4,48,2048]{3,2,0,1:T(8,128)(2,1)}), bf16[8,4,48,2048]{3,2,0,1:T(8,128)(2,1)}, u32[]{:S(2)}, u32[]{:S(2)}) %all-to-all-start.3) | async-done | bytes 6291488 | tf_op jit(solution)/shard_map/all_to_all | solution.py:286
  1279.6 6.6 copy.125
  1286.2 14.4 %gather_fusion.1 = bf16[1280,2048]{1,0:T(8,128)(2,1)} fusion(bf16[1536,2048]{1,0:T(8,128)(2,1)} %bitcast.212, s32[2048]{0:T(1024)S(1)} %pad_clamp_fusion), kind=kCustom, calls=%fused_computation.2 | custom fusion | bytes 10490880 | tf_op jit(solution)/shard_map/gather | solution.py:294
  1300.6 10.3 reshape.217
  1310.9 10.6 multiply_reduce_fusion
  1321.5 2.2 fusion.90
  (266 shorter events, 150.8 us)
Async XLA Ops:
  6.5 1040.0 %copy-start = (bf16[1,512,2048]{2,1,0:T(8,128)(2,1)S(1)}, bf16[1,512,2048]{2,1,0:T(8,128)(2,1)}, u32[]{:S(2)}) copy-start(bf16[1,512,2048]{2,1,0:T(8,128)(2,1)} %param.43) | copy-start | bytes 6291460
  6.5 404.4 %all-gather.6.cloned.1.call-start = ((), (), s32[]{:S(2)}) async-start(), calls=%async_computation.5 | async-start | bytes 2359296 | tf_op jit(solution)/shard_map/all_gather | solution.py:162
  7.4 52.4 %collective-permute-start = (bf16[3,4,512]{2,1,0:T(4,128)(2,1)S(1)}, bf16[3,4,512]{2,1,0:T(4,128)(2,1)S(1)}, u32[]{:S(2)}, u32[]{:S(2)}) collective-permute-start(bf16[3,4,512]{2,1,0:T(4,128)(2,1)S(1)} %slice.61), channel_id=1, source_target_pairs={{0,4},{4,8},{8,12},{12,16},{16,20},{20,24},{24,28},{1,5},{5,9},{9,... | collective-permute-start | bytes 36872 | tf_op jit(solution)/shard_map/ppermute | solution.py:21
  14.1 569.6 %all-gather.8.cloned.1.call-start = ((), (), s32[]{:S(2)}) async-start(), calls=%async_computation.7 | async-start | bytes 2359296 | tf_op jit(solution)/shard_map/all_gather | solution.py:27
  74.7 1.3 copy-start.2
  399.9 2.3 copy-start.3
  402.2 2.3 copy-start.9
  422.4 5.2 copy-start.1
  437.3 5.2 copy-start.1
  452.1 5.2 copy-start.1
  466.9 5.2 copy-start.1
  481.7 5.2 copy-start.1
  496.5 5.2 copy-start.1
  511.4 5.2 copy-start.1
  526.2 5.2 copy-start.1
  533.5 3.8 copy-start.13
  533.5 3.8 copy-start.8
  535.4 98.2 %all-gather.10.cloned.1.call-start = ((), (), s32[]{:S(2)}) async-start(), calls=%async_computation.8 | async-start | bytes 2359296 | tf_op jit(solution)/shard_map/all_gather | solution.py:27
  537.3 245.7 %reduce-scatter.2.cloned.1.call-start = ((), (), s32[]{:S(2)}) async-start(), calls=%async_computation.6 | async-start | bytes 2621440 | tf_op jit(solution)/shard_map/reduce_scatter | solution.py:249
  537.6 2.3 copy-start.4
  733.9 3.6 copy-start.14
  736.9 1.2 copy-start.16
  742.2 0.7 copy-start.10
  742.2 40.7 %copy-start.6 = (bf16[128,2048]{1,0:T(8,128)(2,1)S(1)}, bf16[128,2048]{1,0:T(8,128)(2,1)}, u32[]{:S(2)}) copy-start(bf16[128,2048]{1,0:T(8,128)(2,1)} %param.37) | copy-start | bytes 1572868
  742.2 42.0 %copy-start.12 = (f32[2048]{0:T(1024)S(1)}, f32[2048]{0:T(1024)}, u32[]{:S(2)}) copy-start(f32[2048]{0:T(1024)} %param.38) | copy-start | bytes 24580
  1037.6 3.8 copy-start.15
  1038.8 2.6 copy-start.5
  1203.3 5.6 copy-start.11
  1203.3 76.3 %all-to-all-start.3 = ((bf16[8,4,48,2048]{3,2,0,1:T(8,128)(2,1)}), bf16[8,4,48,2048]{3,2,0,1:T(8,128)(2,1)}, u32[]{:S(2)}, u32[]{:S(2)}) async-start(bf16[8,4,48,2048]{3,2,0,1:T(8,128)(2,1)} %copy.124), calls=%async_computation.4 | async-start | bytes 12582912 | tf_op jit(solution)/shard_map/all_to_all | solution.py:286
  1310.9 10.6 copy-start.7
Sparse Core Ops, SparseCore 0:
  14.2 50.2 all-gather.5
  535.5 48.0 all-gather.7
  585.8 47.7 all-gather.9
  742.4 40.5 reduce-scatter.1
where the time goes:
time: 1340 us; the launch traced here: 1330 us
  blocking collectives  390 us (29%)
  other arithmetic  386 us (29%)
  waiting for transfers between devices  198 us (15%)
  matrix products  184 us (14%)
  local copies, waits for them, and re-layouts  116 us (9%)
  loops' own time  31.6 us (2%)
  between operations  14 us (1%)
    another operation x2, other arithmetic, block_parts(): lax.linalg.triangular_solve(lower_mat, right_side, left_side=True, lower=...  316 us
    all_to_all x1, blocking collectives, local(): lax.all_to_all(outgoing, 'seq', split_axis=0, concat_axis=0, tiled=True)  144 us
    all_to_all x1, blocking collectives, local(): lax.all_to_all(results, 'seq', split_axis=0, concat_axis=0, tiled=True)  142 us
    dot_general x48, matrix products, chain_product(): return jnp.einsum('...ik,...kj->...ij', left, right, precision=precise)  101 us
    all_gather x2, waiting for transfers between devices, entering(): lax.all_gather(a.astype(kind), axis)  88.9 us
    all_to_all x1, blocking collectives, local(): lax.all_to_all(lax.all_to_all(outgoing, 'seq', split_axis=0, concat_axis=...  73.3 us
    all_to_all x1, waiting for transfers between devices, local(): lax.all_to_all(lax.all_to_all(results, 'seq', split_axis=0, concat_axis=0...  70.5 us
    reduce_scatter x1, waiting for transfers between devices, local(): lax.psum_scatter(jnp.dot(rows_in, out_weight, preferred_element_type=jnp....  38.7 us
  transfers between devices with their start and end apart: 6, of which 4 were waited for; matrix products, arithmetic and copies ran while one was open for 28% of the time, Pallas kernels for 0%

commit v1 on v0

v1 whole, which is shorter than its diff:
```python
import math

import jax
import jax.numpy as jnp
from jax import lax
from jax.experimental import pallas as pl
from jax.experimental.pallas import tpu as pltpu
from jax.sharding import PartitionSpec as P

D = 2048
HEAD = 128
GROUP = 2
CONV = 4
BLOCK = 64


PACK = 4
LANES = PACK * BLOCK
VMEM_LIMIT = 56 * 1024 * 1024


def product(left, right, contract):
    return lax.dot_general(left, right, (contract, ((), ())), preferred_element_type=jnp.float32)


def split(value):
    high = value.astype(jnp.bfloat16)
    return (high, (value - high.astype(jnp.float32)).astype(jnp.bfloat16))


def fine(left, right, contract=((1,), (0,))):
    left_high, left_low = split(left)
    right_high, right_low = split(right)
    return (
        product(left_high, right_high, contract)
        + product(left_high, right_low, contract)
        + product(left_low, right_high, contract)
    )


def coarse(left, right, contract=((1,), (0,))):
    return product(left.astype(jnp.bfloat16), right.astype(jnp.bfloat16), contract)


def silu(value):
    return value / (1.0 + jnp.exp(-value))


def parts_kernel(
    x_ref, before_ref, taps_ref, col_ref, row_ref, query_ref, key_ref, weighted_ref, values_ref, mix_ref, ext
):
    ext[0:8, :] = before_ref[0]
    ext[8:, :] = x_ref[...].astype(jnp.float32)
    row_id = lax.broadcasted_iota(jnp.int32, (LANES, LANES), 0)
    col_id = lax.broadcasted_iota(jnp.int32, (LANES, LANES), 1)
    same_head = row_id // BLOCK == col_id // BLOCK
    inclusive = same_head & (row_id >= col_id)
    strict = same_head & (row_id > col_id)
    group_width = (2 + GROUP) * HEAD
    heads = col_ref.shape[1] // BLOCK
    for pack in range(heads // PACK):
        queries, keys, values = [], [], []
        for group in range(PACK // GROUP):
            first = (pack * (PACK // GROUP) + group) * group_width
            columns = slice(first, first + group_width)
            mixed = ext[5 : 5 + BLOCK, columns] * taps_ref[0:1, columns]
            for tap in range(1, CONV):
                mixed = mixed + ext[5 + tap : 5 + tap + BLOCK, columns] * taps_ref[tap : tap + 1, columns]
            mixed = silu(mixed)
            query = mixed[:, :HEAD]
            query = query * (
                lax.rsqrt(jnp.sum(query * query, axis=1, keepdims=True) + 1e-06) / math.sqrt(HEAD)
            )
            key = mixed[:, HEAD : 2 * HEAD]
            key = key * lax.rsqrt(jnp.sum(key * key, axis=1, keepdims=True) + 1e-06)
            queries += [query, query]
            keys += [key, key]
            values += [mixed[:, 2 * HEAD : 3 * HEAD], mixed[:, 3 * HEAD :]]
        query = jnp.concatenate(queries, axis=0)
        key = jnp.concatenate(keys, axis=0)
        value = jnp.concatenate(values, axis=0)
        rows = slice(pack * LANES, (pack + 1) * LANES)
        col = col_ref[0, rows, :]
        running, beta, growth, tail = col[:, 0:1], col[:, 1:2], col[:, 2:3], col[:, 3:4]
        decay = jnp.where(
            inclusive, jnp.exp(jnp.where(inclusive, running - row_ref[0, pack : pack + 1, :], 0.0)), 0.0
        )
        across = ((1,), (1,))
        lower = jnp.where(strict, beta * fine(key, key, across) * decay, 0.0)
        mix_ref[0, rows, :] = (coarse(query, key, across) * decay).astype(jnp.bfloat16)
        inverse = jnp.where(row_id == col_id, 1.0, 0.0) - jnp.where(
            row_id // 2 == col_id // 2, lower, 0.0
        )
        size = 2
        while size < BLOCK:
            joint = (row_id // (2 * size) == col_id // (2 * size)) & (row_id // size != col_id // size)
            between = jnp.where(joint, lower, 0.0)
            inverse = inverse - fine(fine(inverse, between), inverse)
            size *= 2
        solved = fine(
            inverse, jnp.concatenate([(beta * growth) * key, beta * value], axis=1)
        )
        query_ref[0, rows, :] = (growth * query).astype(jnp.bfloat16)
        key_ref[0, rows, :] = tail * key
        weighted_ref[0, rows, :] = solved[:, :HEAD]
        values_ref[0, rows, :] = solved[:, HEAD:]


def maps_kernel(first_ref, slot_ref, key_ref, weighted_ref, values_ref, col_ref, cache_ref, out_ref, total):
    block = pl.program_id(0)
    heads = total.shape[0]

    @pl.when(block == 0)
    def _():
        eye = jnp.where(
            lax.broadcasted_iota(jnp.int32, (HEAD, HEAD), 0)
            == lax.broadcasted_iota(jnp.int32, (HEAD, HEAD), 1),
            1.0,
            0.0,
        )
        for head in range(heads):
            total[head] = jnp.concatenate([eye, jnp.zeros((HEAD, HEAD), jnp.float32)], axis=1)

    @pl.when(first_ref[block] == 1)
    def _():
        for head in range(heads):
            total[head] = jnp.concatenate(
                [jnp.zeros((HEAD, HEAD), jnp.float32), cache_ref[0, head].astype(jnp.float32)], axis=1
            )

    for head in range(heads):
        rows = slice(head * BLOCK, (head + 1) * BLOCK)
        state = total[head]
        fixed = (
            jnp.concatenate([jnp.zeros((BLOCK, HEAD), jnp.float32), values_ref[0, rows, :]], axis=1)
            - fine(weighted_ref[0, rows, :], state)
        )
        last = col_ref[0, head * BLOCK : head * BLOCK + 1, 4:5]
        total[head] = last * state + fine(key_ref[0, rows, :], fixed, ((0,), (0,)))

    @pl.when(block == pl.num_programs(0) - 1)
    def _():
        out_ref[...] = total[...].astype(jnp.bfloat16)


def advance_kernel(
    first_ref, slot_ref, place_ref,
    maps_ref, query_ref, key_ref, weighted_ref, values_ref, mix_ref, col_ref, cache_ref, z_ref, gain_ref,
    out_ref, total,
):
    block = pl.program_id(0)
    heads = total.shape[0]

    @pl.when(block == 0)
    def _():
        total[...] = jnp.zeros_like(total)

        def one(step, carry):
            for head in range(heads):
                both = maps_ref[step, head]
                state_high, state_low = split(total[head])
                transfer = both[:, :HEAD]
                contract = ((1,), (0,))
                total[head] = (
                    product(transfer, state_high, contract)
                    + product(transfer, state_low, contract)
                    + both[:, HEAD:].astype(jnp.float32)
                )
            return carry

        lax.fori_loop(0, place_ref[0], one, 0)

    @pl.when(first_ref[block] == 1)
    def _():
        for head in range(heads):
            total[head] = cache_ref[0, head].astype(jnp.float32)

    for pack in range(heads // PACK):
        fixed_rows, outputs = [], []
        for inner in range(PACK):
            head = pack * PACK + inner
            rows = slice(head * BLOCK, (head + 1) * BLOCK)
            state = total[head]
            fixed = values_ref[0, rows, :] - fine(weighted_ref[0, rows, :], state)
            outputs.append(product(query_ref[0, rows, :], state.astype(jnp.bfloat16), ((1,), (0,))))
            last = col_ref[0, head * BLOCK : head * BLOCK + 1, 4:5]
            total[head] = last * state + fine(key_ref[0, rows, :], fixed, ((0,), (0,)))
            fixed_rows.append(fixed.astype(jnp.bfloat16))
        rows = slice(pack * LANES, (pack + 1) * LANES)
        core = jnp.concatenate(outputs, axis=0) + product(
            mix_ref[0, rows, :], jnp.concatenate(fixed_rows, axis=0), ((1,), (0,))
        )
        core = core * lax.rsqrt(jnp.mean(core * core, axis=1, keepdims=True) + 1e-06) * gain_ref[...]
        for inner in range(PACK):
            columns = slice((pack * PACK + inner) * HEAD, (pack * PACK + inner + 1) * HEAD)
            gate = silu(z_ref[:, columns].astype(jnp.float32))
            out_ref[:, columns] = (core[inner * BLOCK : (inner + 1) * BLOCK] * gate).astype(jnp.bfloat16)


def expert_apply(arrived, expert_gate, expert_up, expert_down):
    flat_rows = arrived.reshape(-1, D)
    gate_part = jnp.dot(flat_rows, expert_gate[0], preferred_element_type=jnp.float32)
    up_part = jnp.dot(flat_rows, expert_up[0], preferred_element_type=jnp.float32)
    hidden = (jax.nn.silu(gate_part) * up_part).astype(jnp.bfloat16)
    result = jnp.dot(hidden, expert_down[0], preferred_element_type=jnp.float32).astype(
        jnp.bfloat16
    )
    return result.reshape(arrived.shape)


def local(
    qkv_input,
    z_gate,
    beta_logit,
    decay_input,
    decay_rate,
    conv_weight,
    cache_state,
    cache_tail,
    block_request,
    cache_owner,
    norm_gain,
    out_weight,
    residual,
    post_gain,
    expert_ids,
    expert_weights,
    expert_gate,
    expert_up,
    expert_down,
):
    seq_len, key_heads, row_width = qkv_input.shape
    blocks = seq_len // BLOCK
    head_count = z_gate.shape[1] // HEAD
    seq_count = lax.axis_size("seq")
    exp_count = lax.axis_size("exp")
    previous = jnp.concatenate([jnp.full((1,), -1, jnp.int32), block_request[:-1]])
    starts_all = block_request != previous
    first_block = lax.axis_index("seq") * blocks
    local_request = lax.dynamic_slice_in_dim(block_request, first_block, blocks, 0)
    local_start = lax.dynamic_slice_in_dim(starts_all, first_block, blocks, 0)
    request_ids = jnp.arange(cache_owner.shape[0], dtype=jnp.int32)
    local_slot = jnp.sum(
        jnp.where(local_request[:, None] == request_ids[None, :], cache_owner[None, :], 0), axis=1
    )
    states_all = lax.all_gather(cache_state.astype(jnp.bfloat16), "seq", axis=0, tiled=True)
    width = key_heads * row_width
    rows_flat = qkv_input.reshape(seq_len, width)
    edge = jnp.concatenate(
        [
            cache_tail.astype(jnp.bfloat16).reshape(-1, width),
            rows_flat[seq_len - (CONV - 1) :],
        ],
        axis=0,
    )
    edges = lax.all_gather(edge, "seq", axis=0)
    tails_all = edges[:, : -(CONV - 1)].reshape(-1, CONV - 1, width)
    place = lax.axis_index("seq")
    rim_rows = lax.dynamic_index_in_dim(
        edges[:, -(CONV - 1) :], jnp.maximum(place - 1, 0), 0, False
    )
    before = jnp.concatenate(
        [rim_rows[None], rows_flat.reshape(blocks, BLOCK, width)[:-1, BLOCK - (CONV - 1) :]], axis=0
    )
    before = jnp.where(local_start[:, None, None], tails_all[local_slot], before)
    before = jnp.pad(before.astype(jnp.float32), ((0, 0), (8 - (CONV - 1), 0), (0, 0)))
    beta = jax.nn.sigmoid(beta_logit).reshape(blocks, BLOCK, head_count).transpose(0, 2, 1)
    log_decay = (
        (-decay_rate[None, :] * jax.nn.softplus(decay_input))
        .reshape(blocks, BLOCK, head_count)
        .transpose(0, 2, 1)
    )
    running = jnp.cumsum(log_decay, axis=-1)
    last = running[..., -1:]
    grown = jnp.exp(last)
    columns = jnp.stack(
        [running, beta, jnp.exp(running), jnp.exp(last - running)]
        + [jnp.broadcast_to(grown, running.shape)] * 4,
        axis=-1,
    ).reshape(blocks, head_count * BLOCK, 8)
    packs = head_count // PACK
    running_rows = running.reshape(blocks, packs, LANES)
    stacked = head_count * BLOCK
    rows_spec = pl.BlockSpec((1, stacked, HEAD), lambda b, *_: (b, 0, 0))
    mix_spec = pl.BlockSpec((1, stacked, LANES), lambda b, *_: (b, 0, 0))
    col_spec = pl.BlockSpec((1, stacked, 8), lambda b, *_: (b, 0, 0))
    cache_spec = pl.BlockSpec(
        (1, head_count, HEAD, HEAD), lambda b, first, slot, *_: (slot[b], 0, 0, 0)
    )
    params = pltpu.CompilerParams(vmem_limit_bytes=VMEM_LIMIT)
    rows_shape = (blocks, stacked, HEAD)
    queries, carried, weighted, new_values, mix = pl.pallas_call(
        parts_kernel,
        grid=(blocks,),
        in_specs=[
            pl.BlockSpec((BLOCK, width), lambda b: (b, 0)),
            pl.BlockSpec((1, 8, width), lambda b: (b, 0, 0)),
            pl.BlockSpec((CONV, width), lambda b: (0, 0)),
            col_spec,
            pl.BlockSpec((1, packs, LANES), lambda b: (b, 0, 0)),
        ],
        out_specs=[rows_spec] * 4 + [mix_spec],
        out_shape=[
            jax.ShapeDtypeStruct(rows_shape, jnp.bfloat16),
            jax.ShapeDtypeStruct(rows_shape, jnp.float32),
            jax.ShapeDtypeStruct(rows_shape, jnp.float32),
            jax.ShapeDtypeStruct(rows_shape, jnp.float32),
            jax.ShapeDtypeStruct((blocks, stacked, LANES), jnp.bfloat16),
        ],
        scratch_shapes=[pltpu.VMEM((8 + BLOCK, width), jnp.float32)],
        compiler_params=params,
        cost_estimate=pl.CostEstimate(
            flops=blocks * packs * 40 * 2 * LANES**3, bytes_accessed=16 * 2**20, transcendentals=0
        ),
    )(rows_flat, before, conv_weight.reshape(CONV, width), columns, running_rows)
    firsts = local_start.astype(jnp.int32)
    own_map = pl.pallas_call(
        maps_kernel,
        grid_spec=pltpu.PrefetchScalarGridSpec(
            num_scalar_prefetch=2,
            grid=(blocks,),
            in_specs=[rows_spec, rows_spec, rows_spec, col_spec, cache_spec],
            out_specs=pl.BlockSpec((head_count, HEAD, 2 * HEAD), lambda b, *_: (0, 0, 0)),
            scratch_shapes=[pltpu.VMEM((head_count, HEAD, 2 * HEAD), jnp.float32)],
        ),
        out_shape=jax.ShapeDtypeStruct((head_count, HEAD, 2 * HEAD), jnp.bfloat16),
        compiler_params=params,
    )(firsts, local_slot, carried, weighted, new_values, columns, states_all)
    maps_all = lax.all_gather(own_map, "seq")
    gated = pl.pallas_call(
        advance_kernel,
        grid_spec=pltpu.PrefetchScalarGridSpec(
            num_scalar_prefetch=3,
            grid=(blocks,),
            in_specs=[
                pl.BlockSpec(maps_all.shape, lambda b, *_: (0, 0, 0, 0), pipeline_mode=pl.Buffered(1)),
                rows_spec,
                rows_spec,
                rows_spec,
                rows_spec,
                mix_spec,
                col_spec,
                cache_spec,
                pl.BlockSpec((BLOCK, head_count * HEAD), lambda b, *_: (b, 0)),
                pl.BlockSpec((1, HEAD), lambda b, *_: (0, 0)),
            ],
            out_specs=pl.BlockSpec((BLOCK, head_count * HEAD), lambda b, *_: (b, 0)),
            scratch_shapes=[pltpu.VMEM((head_count, HEAD, HEAD), jnp.float32)],
        ),
        out_shape=jax.ShapeDtypeStruct(z_gate.shape, jnp.bfloat16),
        compiler_params=params,
    )(
        firsts, local_slot, place.reshape(1),
        maps_all, queries, carried, weighted, new_values, mix, columns, states_all, z_gate, norm_gain[None],
    )
    rows_in = gated
    attn = lax.psum_scatter(
        jnp.dot(rows_in, out_weight, preferred_element_type=jnp.float32).astype(jnp.bfloat16),
        "exp",
        scatter_dimension=0,
        tiled=True,
    ).astype(jnp.float32)
    mid_wide = (residual.astype(jnp.float32) + attn).astype(jnp.bfloat16).astype(jnp.float32)
    normed = (
        mid_wide
        * lax.rsqrt(jnp.mean(mid_wide * mid_wide, axis=-1, keepdims=True) + 1e-06)
        * post_gain
    ).astype(jnp.bfloat16)
    route = expert_weights / jnp.sum(expert_weights, axis=-1, keepdims=True)
    token_count, top_count = expert_ids.shape
    expert_count = seq_count * exp_count
    capacity = max(2, token_count * top_count * 6 // (expert_count * 5))
    names = jnp.arange(expert_count, dtype=expert_ids.dtype)
    chosen = expert_ids[:, :, None] == names
    hot = jnp.any(chosen, axis=1)
    share = jnp.sum(jnp.where(chosen, route[:, :, None], 0.0), axis=1)
    rank = jnp.cumsum(hot.astype(jnp.int32), axis=0) - 1
    placed = hot[:, :, None] & (rank[:, :, None] == jnp.arange(capacity, dtype=jnp.int32))
    flat_placed = placed.astype(jnp.bfloat16).reshape(token_count, expert_count * capacity)
    outgoing = jnp.dot(flat_placed.T, normed, preferred_element_type=jnp.float32).astype(jnp.bfloat16)
    devices = ("seq", "exp")
    arrived = lax.all_to_all(outgoing, devices, split_axis=0, concat_axis=0, tiled=True)
    results = expert_apply(arrived, expert_gate, expert_up, expert_down)
    returned = lax.all_to_all(results, devices, split_axis=0, concat_axis=0, tiled=True)
    share_high, share_low = split(share)
    moe_sum = sum(
        jnp.dot(
            (placed * part[:, :, None]).reshape(token_count, expert_count * capacity),
            returned,
            preferred_element_type=jnp.float32,
        )
        for part in (share_high, share_low)
    )
    return (mid_wide + moe_sum).astype(jnp.bfloat16)


def solution(mesh):
    in_specs = (
        P("seq", "exp", None),
        P("seq", "exp"),
        P("seq", "exp"),
        P("seq", "exp"),
        P("exp"),
        P(None, "exp", None),
        P("seq", "exp", None, None),
        P("seq", None, "exp", None),
        P(),
        P(),
        P(),
        P("exp", None),
        P(("seq", "exp"), None),
        P(),
        P(("seq", "exp"), None),
        P(("seq", "exp"), None),
        P(("seq", "exp"), None, None),
        P(("seq", "exp"), None, None),
        P(("seq", "exp"), None, None),
    )
    out_specs = P(("seq", "exp"), None)
    return jax.shard_map(local, mesh=mesh, in_specs=in_specs, out_specs=out_specs, check_vma=False)
```

time: 1340 us -> 608 us (0.45)
  other arithmetic: 386 us -> 7.49 us
  blocking collectives: 390 us -> 176 us
  matrix products: 184 us -> 33.3 us
  Pallas kernels: 0 us -> 85.8 us
  local copies, waits for them, and re-layouts: 116 us -> 41.3 us
  waiting for transfers between devices: 198 us -> 245 us
  loops' own time: 31.6 us -> 0 us
    another operation x3 -> x2, other arithmetic: 318 us -> 1.94 us  [the longest x1 1.77 us: local(): running = jnp.cumsum(log_decay, axis=-1)]
    all_to_all x3 -> x1, blocking collectives: 359 us -> 143 us  [local(): lax.all_to_all(outgoing, devices, split_axis=0, concat_axis=0, tiled=True)]
    dot_general x74 -> x3, matrix products: 159 us -> 11.5 us  [the longest x2 8.55 us: local(): jnp.dot((placed * part[:, :, None]).reshape(token_count, expert_count * c...]
    pallas_call x0 -> x3, Pallas kernels: none -> 85.8 us  [the longest x1 54.9 us: local(): pl.pallas_call(parts_kernel, grid=(blocks,), in_specs=[pl.BlockSpec((BLOC...]
    all_to_all x1, waiting for transfers between devices: 70.5 us -> 140 us  [local(): lax.all_to_all(results, devices, split_axis=0, concat_axis=0, tiled=True)]
    scatter x1 -> x0, local copies, waits for them, and re-layouts: 34 us -> none  [local(): outgoing = jnp.zeros((expert_count * capacity, D), jnp.bfloat16).at[slot_...]
    another operation x3 -> x0, loops' own time: 31.6 us -> none  [the longest x1 16.4 us: local(): lax.scan(advance, incoming, (growth, weighted_keys, new_values, carried_k...]
    another operation x1 -> x7, local copies, waits for them, and re-layouts: 3.07 us -> 26.4 us  [the longest x6 22 us: local(): jnp.stack([running, beta, jnp.exp(running), jnp.exp(last - running)] + [j...]
  transfers between devices with their start and end apart: 6 -> 4, of which waited for: 4 -> 3; matrix products, arithmetic and copies ran while one was open for 28% -> 7% of each run, Pallas kernels for 0% -> 9%
where the time goes in v1:
time: 608 us; the launch traced here: 607 us
  waiting for transfers between devices  245 us (40%)
  blocking collectives  176 us (29%)
  Pallas kernels  85.8 us (14%)
  local copies, waits for them, and re-layouts  41.3 us (7%)
  matrix products  33.3 us (5%)
  between operations  13.4 us (2%)
  other arithmetic  7.49 us (1%)
    all_to_all x1, blocking collectives, local(): lax.all_to_all(outgoing, devices, split_axis=0, concat_axis=0, tiled=True)  143 us
    all_to_all x1, waiting for transfers between devices, local(): lax.all_to_all(results, devices, split_axis=0, concat_axis=0, tiled=True)  140 us
    all_gather x1, waiting for transfers between devices, local(): maps_all = lax.all_gather(own_map, 'seq')  74.1 us
    pallas_call x1, Pallas kernels, local(): pl.pallas_call(parts_kernel, grid=(blocks,), in_specs=[pl.BlockSpec((BLOC...  54.9 us
    all_gather x1, blocking collectives, local(): edges = lax.all_gather(edge, 'seq', axis=0)  33.1 us
    reduce_scatter x1, waiting for transfers between devices, local(): lax.psum_scatter(jnp.dot(rows_in, out_weight, preferred_element_type=jnp....  31 us
    another operation x6, local copies, waits for them, and re-layouts, local(): jnp.stack([running, beta, jnp.exp(running), jnp.exp(last - running)] + [j...  22 us
    pallas_call x1, Pallas kernels, local(): pl.pallas_call(maps_kernel, grid_spec=pltpu.PrefetchScalarGridSpec(num_sc...  15.5 us
  transfers between devices with their start and end apart: 4, of which 3 were waited for; matrix products, arithmetic and copies ran while one was open for 7% of the time, Pallas kernels for 9%

profile of v1, /device:TPU:0, one launch (start us, length us, event | category | flops | bytes accessed | tf_op | source)
XLA Modules:
  0.0 606.7 jit_solution(10486557550686976684)
XLA Ops:
  6.5 0.0 copy-start.7
  6.6 0.0 all-gather.6.cloned.1.call-start
  6.6 1.9 convert_element_type.79
  8.5 0.0 all-gather.6.cloned.1.call-update
  8.6 0.0 all-gather.8.cloned.1.call-start
  8.6 0.7 slice_bitcast_fusion
  9.3 4.4 reshape_reshape.3
  13.8 0.0 copy-done.8
  13.8 0.1 fusion.31
  13.8 0.1 reshape.135
  13.9 1.8 reduce_window_sum.22
  15.7 0.2 exponential_reduce_fusion
  15.9 0.1 stack.11
  16.0 0.7 reshape.137.row_ref
  16.6 0.1 dynamic_slice.11
  16.7 0.2 select_reduce_fusion.1.slot_ref
  17.0 33.1 %all-gather.2 = bf16[8,6,2048]{2,1,0:T(8,128)(2,1)S(1)} all-gather(bf16[1,6,2048]{2,1,0:T(8,128)(2,1)S(1)} %maximum_bitcast_fusion), channel_id=2, replica_groups=mesh['seq'=8,'exp'=4] {'seq'}, dimensions={0}, use_global_device_ids=true | all-gather | bytes 221184 | tf_op jit(solution)/shard_map/all_gather | solution.py:256
  50.1 1.0 slice.32
  51.1 0.1 sub.36
  51.2 0.1 sub.37
  51.3 2.0 copy.73
  53.3 0.0 copy-start.9
  53.3 2.0 copy.75
  55.2 2.0 copy.76
  57.2 0.1 stack_broadcast_in_dim.4
  57.3 3.4 stack_broadcast_in_dim.6
  60.7 0.1 reshape.136
  60.8 0.0 copy-start.4
  60.8 3.4 stack.14
  64.3 3.5 copy.83
  67.8 0.6 copy.86
  68.5 0.1 fusion.37
  68.6 0.7 gather_fusion
  69.2 13.0 %stack.13.col_ref = f32[8,512,8]{2,1,0:T(8,128)} concatenate(f32[8,512,1]{2,1,0:T(8,128)} %copy.73, f32[8,512,1]{2,1,0:T(8,128)} %stack.14, f32[8,512,1]{2,1,0:T(8,128)} %copy.75, f32[8,512,1]{2,1,0:T(8,128)} %copy.76, f32[8,512,1]{2,1,0:T(8,128)} %stack_broadcast_in_dim.6, f32[8,512,1]{2,1,0:T(8,128)} %stack_broadcast_in_dim.6, f32[8,512,1]{2,1,0:T(8,128)} %stack_broadcast_in_dim.6, ...), dimensions={2} | concatenate | bytes 262144 | tf_op jit(solution)/shard_map/stack | solution.py:276
  82.3 0.1 add_compare_fusion
  82.4 0.6 fusion.36
  82.9 0.1 maximum_select_fusion
  83.1 0.9 pad_convert_fusion.before_ref
  83.9 54.9 %shard_map.181 = (bf16[8,512,128]{2,1,0:T(8,128)(2,1)}, f32[8,512,128]{2,1,0:T(8,128)}, f32[8,512,128]{2,1,0:T(8,128)}, f32[8,512,128]{2,1,0:T(8,128)}, bf16[8,512,256]{2,1,0:T(8,128)(2,1)}) custom-call(bf16[512,2048]{1,0:T(8,128)(2,1)} %bitcast.74, f32[8,8,2048]{2,1,0:T(8,128)} %pad_convert_fusion.before_ref, f32[4,2048]{1,0:T(4,128)} %bitcast.80, ...), custom_call_target="tpu_custom_call" | custom-call | flops 21474836480 | bytes 16777216 | tf_op jit(solution)/shard_map/pallas_call | solution.py:292
  138.9 15.5 %shard_map.182 = bf16[8,128,256]{2,1,0:T(8,128)(2,1)} custom-call(s32[8]{0:T(128)} %get-tuple-element.19.first_ref, s32[8]{0:T(128)} %copy-done.11, f32[8,512,128]{2,1,0:T(8,128)} %get-tuple-element.10.key_ref, f32[8,512,128]{2,1,0:T(8,128)} %get-tuple-element.11.weighted_ref, f32[8,512,128]{2,1,0:T(8,128)} %get-tuple-element.12.values_ref, ...), custom_call_target="tpu_custom_call" | custom-call | tf_op jit(solution)/shard_map/pallas_call | solution.py:317
  154.4 0.0 all-gather.8.cloned.1.call-update
  154.4 0.2 reduce-scatter.2.cloned.1.call-start
  154.6 74.1 %all-gather.8.cloned.1.call-done = bf16[64,128,256]{2,1,0:T(8,128)(2,1)} async-done(((bf16[8,128,256]{2,1,0:T(8,128)(2,1)}), bf16[64,128,256]{2,1,0:T(8,128)(2,1)}) %all-gather.8.cloned.1.call-update) | async-done | bytes 4194320 | tf_op jit(solution)/shard_map/all_gather | solution.py:329
  228.7 15.4 %shard_map.183 = bf16[512,1024]{1,0:T(8,128)(2,1)} custom-call(s32[8]{0:T(128)} %get-tuple-element.19.first_ref, s32[8]{0:T(128)} %copy-done.11, s32[1]{0:T(128)} %bitcast.place_ref, bf16[8,8,128,256]{3,2,1,0:T(8,128)(2,1)} %bitcast.73, bf16[8,512,128]{2,1,0:T(8,128)(2,1)} %get-tuple-element.13.query_ref, f32[8,512,128]{2,1,0:T(8,128)} %get-tuple-element.10.key_ref, ...), custom_call_target="tpu_custom_call" | custom-call | tf_op jit(solution)/shard_map/pallas_call | solution.py:330
  244.1 0.0 copy-start.6
  244.1 4.9 convolution_convert_fusion.2
  249.0 0.0 reduce-scatter.2.cloned.1.call-update
  249.1 0.1 copy.81
  249.2 0.2 reduce_window_sum.23
  249.4 0.1 copy.82
  249.5 0.1 eq.61
  249.6 0.3 fusion.14
  249.9 31.0 %reduce-scatter.2.cloned.1.call-done = bf16[128,2048]{1,0:T(8,128)(2,1)} async-done(((bf16[512,2048]{1,0:T(8,128)(2,1)}), bf16[128,2048]{1,0:T(8,128)(2,1)}) %reduce-scatter.2.cloned.1.call-update) | async-done | bytes 524304 | tf_op jit(solution)/shard_map/reduce_scatter | solution.py:357
  280.8 1.3 fusion.8
  282.2 2.9 convolution_convert_fusion.1
  285.1 0.0 copy-start.14
  285.1 143.0 %all_to_all.21 = bf16[32,48,2048]{2,1,0:T(8,128)(2,1)S(1)} all-to-all(bf16[32,48,2048]{2,1,0:T(8,128)(2,1)S(1)} %bitcast.68), channel_id=1, replica_groups=mesh['seq'=8,'exp'=4] {'seq','exp'}, dimensions={0} | all-to-all | bytes 12582912 | tf_op jit(solution)/shard_map/all_to_all | solution.py:382
  428.1 2.6 copy-done.1
  430.8 5.1 fusion.6
  435.9 11.8 %convolution_convert_fusion = bf16[1536,2048]{1,0:T(8,128)(2,1)} fusion(bf16[1,512,2048]{2,1,0:T(8,128)(2,1)S(1)} %copy-done, bf16[1536,2048]{1,0:T(8,128)(2,1)} %bitcast.72, f32[1536,512]{1,0:T(8,128)} %fusion.6, bf16[1,2048,512]{2,1,0:T(8,128)(2,1)} %param.36), kind=kOutput, calls=%fused_computation.1 | convolution fusion | flops 6450315264 | bytes 19922944 | tf_op jit(solution)/shard_map/dot_general | solution.py:205
  447.7 3.8 all-to-all-start.1
  451.6 139.9 %all-to-all-done.1 = bf16[32,48,2048]{2,1,0:T(8,128)(2,1)} async-done(((bf16[32,48,2048]{2,1,0:T(8,128)(2,1)}), bf16[32,48,2048]{2,1,0:T(8,128)(2,1)}, u32[]{:S(2)}, u32[]{:S(2)}) %all-to-all-start.1) | async-done | bytes 6291488 | tf_op jit(solution)/shard_map/all_to_all | solution.py:384
  591.6 3.9 convolution_bitcast_fusion
  595.5 4.7 fusion.3
  (49 shorter events, 0.3 us)
Async XLA Ops:
  6.5 429.4 %copy-start = (bf16[1,512,2048]{2,1,0:T(8,128)(2,1)S(1)}, bf16[1,512,2048]{2,1,0:T(8,128)(2,1)}, u32[]{:S(2)}) copy-start(bf16[1,512,2048]{2,1,0:T(8,128)(2,1)} %param.37) | copy-start | bytes 6291460
  6.5 7.2 %copy-start.15 = (f32[8]{0:T(128)S(1)}, f32[8]{0:T(128)}, u32[]{:S(2)}) copy-start(f32[8]{0:T(128)} %param.23) | copy-start | bytes 100
  6.5 7.2 %copy-start.8 = (f32[512,8]{0,1:T(8,128)S(1)}, f32[512,8]{0,1:T(8,128)}, u32[]{:S(2)}) copy-start(f32[512,8]{0,1:T(8,128)} %param.22) | copy-start | bytes 49156
  6.5 10.1 %copy-start.12 = (s32[64]{0:T(128)S(1)}, s32[64]{0:T(128)}, u32[]{:S(2)}) copy-start(s32[64]{0:T(128)} %param.27) | copy-start | bytes 772
  6.5 10.2 %copy-start.16 = (s32[8]{0:T(128)S(1)}, s32[8]{0:T(128)}, u32[]{:S(2)}) copy-start(s32[8]{0:T(128)} %param.28) | copy-start | bytes 100
  6.5 10.4 %copy-start.7 = (f32[1,3,4,512]{3,2,1,0:T(4,128)S(1)}, f32[1,3,4,512]{3,2,1,0:T(4,128)}, u32[]{:S(2)}) copy-start(f32[1,3,4,512]{3,2,1,0:T(4,128)} %param.26) | copy-start | bytes 73732
  6.6 132.3 %all-gather.6.cloned.1.call-start = ((), (), s32[]{:S(2)}) async-start(), calls=%async_computation.3 | async-start | bytes 2359296 | tf_op jit(solution)/shard_map/all_gather | solution.py:246
  8.6 220.2 %all-gather.8.cloned.1.call-start = ((), (), s32[]{:S(2)}) async-start(), calls=%async_computation.5 | async-start | bytes 4718592 | tf_op jit(solution)/shard_map/all_gather | solution.py:329
  16.9 40.3 %copy-start.11 = (s32[8]{0:T(128)}, s32[8]{0:T(128)S(1)}, u32[]{:S(2)}) copy-start(s32[8]{0:T(128)S(1)} %select_reduce_fusion.1.slot_ref) | copy-start | bytes 100
  53.3 7.4 %copy-start.9 = (f32[512,8]{0,1:T(8,128)S(1)}, f32[512,8]{0,1:T(8,128)}, u32[]{:S(2)}) copy-start(f32[512,8]{0,1:T(8,128)} %param.21) | copy-start | bytes 49156
  60.8 7.0 %copy-start.4 = (f32[4,4,512]{2,1,0:T(4,128)S(1)}, f32[4,4,512]{2,1,0:T(4,128)}, u32[]{:S(2)}) copy-start(f32[4,4,512]{2,1,0:T(4,128)} %param.24) | copy-start | bytes 98308
  154.4 126.5 %reduce-scatter.2.cloned.1.call-start = ((), (), s32[]{:S(2)}) async-start(), calls=%async_computation.4 | async-start | bytes 2621440 | tf_op jit(solution)/shard_map/reduce_scatter | solution.py:357
  228.7 15.4 %copy-start.13 = (bf16[1024,2048]{1,0:T(8,128)(2,1)S(1)}, bf16[1024,2048]{1,0:T(8,128)(2,1)}, u32[]{:S(2)}) copy-start(bf16[1024,2048]{1,0:T(8,128)(2,1)} %param.30) | copy-start | bytes 12582916
  244.1 4.9 copy-start.6
  249.0 31.8 %copy-start.2 = (bf16[128,2048]{1,0:T(8,128)(2,1)S(1)}, bf16[128,2048]{1,0:T(8,128)(2,1)}, u32[]{:S(2)}) copy-start(bf16[128,2048]{1,0:T(8,128)(2,1)} %param.31) | copy-start | bytes 1572868
  249.0 33.1 %copy-start.10 = (f32[2048]{0:T(1024)S(1)}, f32[2048]{0:T(1024)}, u32[]{:S(2)}) copy-start(f32[2048]{0:T(1024)} %param.32) | copy-start | bytes 24580
  285.1 145.7 %copy-start.14 = (bf16[1,2048,512]{2,1,0:T(8,128)(2,1)S(1)}, bf16[1,2048,512]{2,1,0:T(8,128)(2,1)}, u32[]{:S(2)}) copy-start(bf16[1,2048,512]{2,1,0:T(8,128)(2,1)} %param.35) | copy-start | bytes 6291460
  428.1 2.6 copy-start.1
  447.7 3.8 copy-start.5
  447.7 143.9 %all-to-all-start.1 = ((bf16[32,48,2048]{2,1,0:T(8,128)(2,1)}), bf16[32,48,2048]{2,1,0:T(8,128)(2,1)}, u32[]{:S(2)}, u32[]{:S(2)}) async-start(bf16[32,48,2048]{2,1,0:T(8,128)(2,1)} %bitcast.70), calls=%async_computation.2 | async-start | bytes 12582912 | tf_op jit(solution)/shard_map/all_to_all | solution.py:384
  591.6 3.9 copy-start.3
Sparse Core Ops, SparseCore 0:
  9.5 53.6 all-gather.5
  154.5 74.1 all-gather.7
  249.2 31.6 reduce-scatter.1

commit v2 on v1

--- a/solution.py
+++ b/solution.py
@@ -14,7 +14,7 @@
 BLOCK = 64
 
 
-PACK = 4
+PACK = 2
 LANES = PACK * BLOCK
 VMEM_LIMIT = 56 * 1024 * 1024
 
@@ -47,7 +47,7 @@
 
 
 def parts_kernel(
-    x_ref, before_ref, taps_ref, col_ref, row_ref, query_ref, key_ref, weighted_ref, values_ref, mix_ref, ext
+    x_ref, before_ref, taps_ref, row_ref, query_ref, key_ref, weighted_ref, values_ref, mix_ref, ext
 ):
     ext[0:8, :] = before_ref[0]
     ext[8:, :] = x_ref[...].astype(jnp.float32)
@@ -57,7 +57,8 @@
     inclusive = same_head & (row_id >= col_id)
     strict = same_head & (row_id > col_id)
     group_width = (2 + GROUP) * HEAD
-    heads = col_ref.shape[1] // BLOCK
+    heads = row_ref.shape[2] // BLOCK
+    cols = row_ref[0].T
     for pack in range(heads // PACK):
         queries, keys, values = [], [], []
         for group in range(PACK // GROUP):
@@ -80,10 +81,10 @@
         key = jnp.concatenate(keys, axis=0)
         value = jnp.concatenate(values, axis=0)
         rows = slice(pack * LANES, (pack + 1) * LANES)
-        col = col_ref[0, rows, :]
+        col = cols[rows, :]
         running, beta, growth, tail = col[:, 0:1], col[:, 1:2], col[:, 2:3], col[:, 3:4]
         decay = jnp.where(
-            inclusive, jnp.exp(jnp.where(inclusive, running - row_ref[0, pack : pack + 1, :], 0.0)), 0.0
+            inclusive, jnp.exp(jnp.where(inclusive, running - row_ref[0, 0:1, rows], 0.0)), 0.0
         )
         across = ((1,), (1,))
         lower = jnp.where(strict, beta * fine(key, key, across) * decay, 0.0)
@@ -135,7 +136,7 @@
             jnp.concatenate([jnp.zeros((BLOCK, HEAD), jnp.float32), values_ref[0, rows, :]], axis=1)
             - fine(weighted_ref[0, rows, :], state)
         )
-        last = col_ref[0, head * BLOCK : head * BLOCK + 1, 4:5]
+        last = col_ref[0, 4:5, head * BLOCK : head * BLOCK + 1]
         total[head] = last * state + fine(key_ref[0, rows, :], fixed, ((0,), (0,)))
 
     @pl.when(block == pl.num_programs(0) - 1)
@@ -143,8 +144,37 @@
         out_ref[...] = total[...].astype(jnp.bfloat16)
 
 
+def enter_kernel(maps_ref, out_ref, state):
+    @pl.when(pl.program_id(0) == 0)
+    def _():
+        state[...] = jnp.zeros_like(state)
+
+    for head in range(state.shape[0]):
+        both = maps_ref[0, head]
+        out_ref[0, head] = state[head].astype(jnp.bfloat16)
+        high, low = split(state[head])
+        contract = ((1,), (0,))
+        state[head] = (
+            product(both[:, :HEAD], high, contract)
+            + product(both[:, :HEAD], low, contract)
+            + both[:, HEAD:].astype(jnp.float32)
+        )
+
+
+def enter_states(maps):
+    shards, heads = maps.shape[:2]
+    return pl.pallas_call(
+        enter_kernel,
+        grid=(shards,),
+        in_specs=[pl.BlockSpec((1, heads, HEAD, 2 * HEAD), lambda step: (step, 0, 0, 0))],
+        out_specs=pl.BlockSpec((1, heads, HEAD, HEAD), lambda step: (step, 0, 0, 0)),
+        out_shape=jax.ShapeDtypeStruct((shards, heads, HEAD, HEAD), jnp.bfloat16),
+        scratch_shapes=[pltpu.VMEM((heads, HEAD, HEAD), jnp.float32)],
+    )(maps)
+
+
 def advance_kernel(
-    first_ref, slot_ref, place_ref,
+    first_ref, slot_ref,
     maps_ref, query_ref, key_ref, weighted_ref, values_ref, mix_ref, col_ref, cache_ref, z_ref, gain_ref,
     out_ref, total,
 ):
@@ -153,22 +183,7 @@
 
     @pl.when(block == 0)
     def _():
-        total[...] = jnp.zeros_like(total)
-
-        def one(step, carry):
-            for head in range(heads):
-                both = maps_ref[step, head]
-                state_high, state_low = split(total[head])
-                transfer = both[:, :HEAD]
-                contract = ((1,), (0,))
-                total[head] = (
-                    product(transfer, state_high, contract)
-                    + product(transfer, state_low, contract)
-                    + both[:, HEAD:].astype(jnp.float32)
-                )
-            return carry
-
-        lax.fori_loop(0, place_ref[0], one, 0)
+        total[...] = maps_ref[...].astype(jnp.float32)
 
     @pl.when(first_ref[block] == 1)
     def _():
@@ -183,7 +198,7 @@
             state = total[head]
             fixed = values_ref[0, rows, :] - fine(weighted_ref[0, rows, :], state)
             outputs.append(product(query_ref[0, rows, :], state.astype(jnp.bfloat16), ((1,), (0,))))
-            last = col_ref[0, head * BLOCK : head * BLOCK + 1, 4:5]
+            last = col_ref[0, 4:5, head * BLOCK : head * BLOCK + 1]
             total[head] = last * state + fine(key_ref[0, rows, :], fixed, ((0,), (0,)))
             fixed_rows.append(fixed.astype(jnp.bfloat16))
         rows = slice(pack * LANES, (pack + 1) * LANES)
@@ -253,7 +268,9 @@
         ],
         axis=0,
     )
-    edges = lax.all_gather(edge, "seq", axis=0)
+    edges = lax.all_to_all(
+        jnp.broadcast_to(edge[None], (seq_count,) + edge.shape), "seq", 0, 0, tiled=True
+    )
     tails_all = edges[:, : -(CONV - 1)].reshape(-1, CONV - 1, width)
     place = lax.axis_index("seq")
     rim_rows = lax.dynamic_index_in_dim(
@@ -276,14 +293,13 @@
     columns = jnp.stack(
         [running, beta, jnp.exp(running), jnp.exp(last - running)]
         + [jnp.broadcast_to(grown, running.shape)] * 4,
-        axis=-1,
-    ).reshape(blocks, head_count * BLOCK, 8)
+        axis=1,
+    ).reshape(blocks, 8, head_count * BLOCK)
     packs = head_count // PACK
-    running_rows = running.reshape(blocks, packs, LANES)
     stacked = head_count * BLOCK
     rows_spec = pl.BlockSpec((1, stacked, HEAD), lambda b, *_: (b, 0, 0))
     mix_spec = pl.BlockSpec((1, stacked, LANES), lambda b, *_: (b, 0, 0))
-    col_spec = pl.BlockSpec((1, stacked, 8), lambda b, *_: (b, 0, 0))
+    col_spec = pl.BlockSpec((1, 8, stacked), lambda b, *_: (b, 0, 0))
     cache_spec = pl.BlockSpec(
         (1, head_count, HEAD, HEAD), lambda b, first, slot, *_: (slot[b], 0, 0, 0)
     )
@@ -297,7 +313,6 @@
             pl.BlockSpec((1, 8, width), lambda b: (b, 0, 0)),
             pl.BlockSpec((CONV, width), lambda b: (0, 0)),
             col_spec,
-            pl.BlockSpec((1, packs, LANES), lambda b: (b, 0, 0)),
         ],
         out_specs=[rows_spec] * 4 + [mix_spec],
         out_shape=[
@@ -312,7 +327,7 @@
         cost_estimate=pl.CostEstimate(
             flops=blocks * packs * 40 * 2 * LANES**3, bytes_accessed=16 * 2**20, transcendentals=0
         ),
-    )(rows_flat, before, conv_weight.reshape(CONV, width), columns, running_rows)
+    )(rows_flat, before, conv_weight.reshape(CONV, width), columns)
     firsts = local_start.astype(jnp.int32)
     own_map = pl.pallas_call(
         maps_kernel,
@@ -326,14 +341,28 @@
         out_shape=jax.ShapeDtypeStruct((head_count, HEAD, 2 * HEAD), jnp.bfloat16),
         compiler_params=params,
     )(firsts, local_slot, carried, weighted, new_values, columns, states_all)
-    maps_all = lax.all_gather(own_map, "seq")
+    if head_count % seq_count == 0:
+        swapped = lax.all_to_all(own_map, "seq", 0, 0, tiled=True)
+        incoming = lax.all_to_all(
+            enter_states(swapped.reshape(seq_count, -1, HEAD, 2 * HEAD)).reshape(
+                head_count, HEAD, HEAD
+            ),
+            "seq",
+            0,
+            0,
+            tiled=True,
+        )
+    else:
+        incoming = lax.dynamic_index_in_dim(
+            enter_states(lax.all_gather(own_map, "seq")), place, 0, False
+        )
     gated = pl.pallas_call(
         advance_kernel,
         grid_spec=pltpu.PrefetchScalarGridSpec(
-            num_scalar_prefetch=3,
+            num_scalar_prefetch=2,
             grid=(blocks,),
             in_specs=[
-                pl.BlockSpec(maps_all.shape, lambda b, *_: (0, 0, 0, 0), pipeline_mode=pl.Buffered(1)),
+                pl.BlockSpec((head_count, HEAD, HEAD), lambda b, *_: (0, 0, 0)),
                 rows_spec,
                 rows_spec,
                 rows_spec,
@@ -350,8 +379,8 @@
         out_shape=jax.ShapeDtypeStruct(z_gate.shape, jnp.bfloat16),
         compiler_params=params,
     )(
-        firsts, local_slot, place.reshape(1),
-        maps_all, queries, carried, weighted, new_values, mix, columns, states_all, z_gate, norm_gain[None],
+        firsts, local_slot,
+        incoming, queries, carried, weighted, new_values, mix, columns, states_all, z_gate, norm_gain[None],
     )
     rows_in = gated
     attn = lax.psum_scatter(

time: 608 us -> 528 us (0.87)
  waiting for transfers between devices: 245 us -> 170 us
  local copies, waits for them, and re-layouts: 41.3 us -> 17.3 us
  Pallas kernels: 85.8 us -> 94.5 us
  starting transfers between devices: 4.13 us -> 11.2 us
    all_gather x1 -> x0, waiting for transfers between devices: 74.1 us -> none  [local(): maps_all = lax.all_gather(own_map, 'seq')]
    all_gather x1 -> x0, blocking collectives: 33.1 us -> none  [local(): edges = lax.all_gather(edge, 'seq', axis=0)]
    all_to_all x0 -> x2, blocking collectives: none -> 32.2 us  [the longest x1 19.9 us: local(): swapped = lax.all_to_all(own_map, 'seq', 0, 0, tiled=True)]
    another operation x6 -> x5, local copies, waits for them, and re-layouts: 22 us -> 1.16 us  [local(): jnp.stack([running, beta, jnp.exp(running), jnp.exp(last - running)] + [j...]
    all_to_all x0 -> x1, starting transfers between devices: none -> 7.28 us  [local(): lax.all_to_all(jnp.broadcast_to(edge[None], (seq_count,) + edge.shape), '...]
    pallas_call x1, Pallas kernels: 54.9 us -> 61 us  [local(): pl.pallas_call(parts_kernel, grid=(blocks,), in_specs=[pl.BlockSpec((BLOC...]
  transfers between devices with their start and end apart: 4 -> 4, of which waited for: 3 -> 2; matrix products, arithmetic and copies ran while one was open for 7% -> 4% of each run, Pallas kernels for 9% -> 12%
where the time goes in v2:
time: 528 us; the launch traced here: 527 us
  blocking collectives  175 us (33%)
  waiting for transfers between devices  170 us (32%)
  Pallas kernels  94.5 us (18%)
  matrix products  33.3 us (6%)
  local copies, waits for them, and re-layouts  17.3 us (3%)
  between operations  13.6 us (3%)
  other arithmetic  11.8 us (2%)
  starting transfers between devices  11.2 us (2%)
    all_to_all x1, blocking collectives, local(): lax.all_to_all(outgoing, devices, split_axis=0, concat_axis=0, tiled=True)  143 us
    all_to_all x1, waiting for transfers between devices, local(): lax.all_to_all(results, devices, split_axis=0, concat_axis=0, tiled=True)  140 us
    pallas_call x1, Pallas kernels, local(): pl.pallas_call(parts_kernel, grid=(blocks,), in_specs=[pl.BlockSpec((BLOC...  61 us
    reduce_scatter x1, waiting for transfers between devices, local(): lax.psum_scatter(jnp.dot(rows_in, out_weight, preferred_element_type=jnp....  29.6 us
    all_to_all x1, blocking collectives, local(): swapped = lax.all_to_all(own_map, 'seq', 0, 0, tiled=True)  19.9 us
    pallas_call x1, Pallas kernels, local(): pl.pallas_call(maps_kernel, grid_spec=pltpu.PrefetchScalarGridSpec(num_sc...  15.1 us
    pallas_call x1, Pallas kernels, local(): pl.pallas_call(advance_kernel, grid_spec=pltpu.PrefetchScalarGridSpec(num...  13.4 us
    all_to_all x1, blocking collectives, local(): lax.all_to_all(enter_states(swapped.reshape(seq_count, -1, HEAD, 2 * HEAD...  12.3 us
  transfers between devices with their start and end apart: 4, of which 2 were waited for; matrix products, arithmetic and copies ran while one was open for 4% of the time, Pallas kernels for 12%

profile of v2, /device:TPU:0, one launch (start us, length us, event | category | flops | bytes accessed | tf_op | source)
XLA Modules:
  0.0 526.6 jit_solution(7893903192829935567)
XLA Ops:
  6.5 0.0 copy-start
  6.5 0.0 all-gather.2.cloned.1.call-start
  6.5 1.9 convert_element_type.79
  8.5 0.0 all-gather.2.cloned.1.call-update
  8.5 0.7 convert_bitcast_fusion
  9.3 0.7 slice_bitcast_fusion
  10.0 0.7 broadcast_in_dim.35
  10.7 7.3 %all-to-all-start = ((bf16[8,6,2048]{2,1,0:T(8,128)(2,1)}), bf16[8,6,2048]{2,1,0:T(8,128)(2,1)S(1)}, u32[]{:S(2)}, u32[]{:S(2)}) async-start(bf16[8,6,2048]{2,1,0:T(8,128)(2,1)} %broadcast_in_dim.35), calls=%async_computation | async-start | bytes 524288 | tf_op jit(solution)/shard_map/all_to_all | solution.py:271
  18.0 0.0 reduce-scatter.2.cloned.1.call-start
  18.1 0.7 neg.15
  18.7 0.8 fusion.31
  19.5 0.1 reshape.145
  19.6 1.8 reduce_window_sum.22
  21.4 0.1 stack.11
  21.5 0.2 exponential_reduce_fusion
  21.6 0.1 sub.36
  21.7 0.1 sub.37
  21.8 0.7 dynamic_slice.11
  22.5 0.8 select_reduce_fusion.1.slot_ref
  23.4 0.8 add_compare_fusion
  24.2 0.7 add_divide_fusion
  24.9 0.6 fusion.36
  25.5 4.5 reshape_reshape.3
  30.0 1.0 slice.32
  31.0 0.1 stack_broadcast_in_dim.7
  31.1 0.1 stack_broadcast_in_dim.8
  31.2 0.1 reshape.146
  31.3 0.1 stack.12
  31.4 3.6 copy.42
  35.0 0.6 copy.45
  35.6 0.8 stack.13.row_ref.col_ref
  36.4 0.0 all-to-all-done
  36.5 0.1 fusion.37
  36.6 0.7 gather_fusion
  37.3 0.1 maximum_select_fusion
  37.4 0.9 pad_convert_fusion.before_ref
  38.3 61.0 %shard_map.181 = (bf16[8,512,128]{2,1,0:T(8,128)(2,1)}, f32[8,512,128]{2,1,0:T(8,128)}, f32[8,512,128]{2,1,0:T(8,128)}, f32[8,512,128]{2,1,0:T(8,128)}, bf16[8,512,128]{2,1,0:T(8,128)(2,1)}) custom-call(bf16[512,2048]{1,0:T(8,128)(2,1)} %bitcast.75, f32[8,8,2048]{2,1,0:T(8,128)} %pad_convert_fusion.before_ref, f32[4,2048]{1,0:T(4,128)} %bitcast.87, ...), custom_call_target="tpu_custom_call" | custom-call | flops 5368709120 | bytes 16777216 | tf_op jit(solution)/shard_map/pallas_call | solution.py:308
  99.3 15.1 %shard_map.182 = bf16[8,128,256]{2,1,0:T(8,128)(2,1)} custom-call(s32[8]{0:T(128)} %get-tuple-element.19.first_ref, s32[8]{0:T(128)} %copy-done.8, f32[8,512,128]{2,1,0:T(8,128)} %get-tuple-element.10.key_ref, f32[8,512,128]{2,1,0:T(8,128)} %get-tuple-element.11.weighted_ref, f32[8,512,128]{2,1,0:T(8,128)} %get-tuple-element.12.values_ref, ...), custom_call_target="tpu_custom_call" | custom-call | tf_op jit(solution)/shard_map/pallas_call | solution.py:332
  114.4 19.9 %all_to_all.36 = bf16[8,128,256]{2,1,0:T(8,128)(2,1)} all-to-all(bf16[8,128,256]{2,1,0:T(8,128)(2,1)} %shard_map.182), channel_id=1, replica_groups=mesh['seq'=8,'exp'=4] {'seq'}, dimensions={0} | all-to-all | bytes 1048576 | tf_op jit(solution)/shard_map/all_to_all | solution.py:345
  134.3 5.0 shard_map.183
  139.3 12.3 %all_to_all.37.maps_ref = bf16[8,128,128]{2,1,0:T(8,128)(2,1)} all-to-all(bf16[8,128,128]{2,1,0:T(8,128)(2,1)} %bitcast.77), channel_id=1, replica_groups=mesh['seq'=8,'exp'=4] {'seq'}, dimensions={0} | all-to-all | bytes 524288 | tf_op jit(solution)/shard_map/all_to_all | solution.py:346
  151.6 13.4 %shard_map.184 = bf16[512,1024]{1,0:T(8,128)(2,1)} custom-call(s32[8]{0:T(128)} %get-tuple-element.19.first_ref, s32[8]{0:T(128)} %copy-done.8, bf16[8,128,128]{2,1,0:T(8,128)(2,1)} %all_to_all.37.maps_ref, bf16[8,512,128]{2,1,0:T(8,128)(2,1)} %get-tuple-element.13.query_ref, f32[8,512,128]{2,1,0:T(8,128)} %get-tuple-element.10.key_ref, ...), custom_call_target="tpu_custom_call" | custom-call | tf_op jit(solution)/shard_map/pallas_call | solution.py:359
  165.1 0.0 copy-start.6
  165.1 4.9 convolution_convert_fusion.2
  170.0 0.0 reduce-scatter.2.cloned.1.call-update
  170.1 0.1 copy.40
  170.2 0.2 reduce_window_sum.23
  170.3 0.1 copy.41
  170.4 0.1 eq.61
  170.5 0.3 fusion.14
  170.8 29.6 %reduce-scatter.2.cloned.1.call-done = bf16[128,2048]{1,0:T(8,128)(2,1)} async-done(((bf16[512,2048]{1,0:T(8,128)(2,1)}), bf16[128,2048]{1,0:T(8,128)(2,1)}) %reduce-scatter.2.cloned.1.call-update) | async-done | bytes 524304 | tf_op jit(solution)/shard_map/reduce_scatter | solution.py:386
  200.4 1.3 fusion.8
  201.7 2.9 convolution_convert_fusion.1
  204.6 0.0 copy-start.10
  204.6 143.0 %all_to_all.38 = bf16[32,48,2048]{2,1,0:T(8,128)(2,1)S(1)} all-to-all(bf16[32,48,2048]{2,1,0:T(8,128)(2,1)S(1)} %bitcast.70), channel_id=1, replica_groups=mesh['seq'=8,'exp'=4] {'seq','exp'}, dimensions={0} | all-to-all | bytes 12582912 | tf_op jit(solution)/shard_map/all_to_all | solution.py:411
  347.6 2.7 copy-done.1
  350.3 0.0 copy-done.10
  350.3 5.2 fusion.6
  355.5 11.8 %convolution_convert_fusion = bf16[1536,2048]{1,0:T(8,128)(2,1)} fusion(bf16[1,512,2048]{2,1,0:T(8,128)(2,1)S(1)} %copy-done, bf16[1536,2048]{1,0:T(8,128)(2,1)} %bitcast.74, f32[1536,512]{1,0:T(8,128)} %fusion.6, bf16[1,2048,512]{2,1,0:T(8,128)(2,1)} %param.36), kind=kOutput, calls=%fused_computation.1 | convolution fusion | flops 6450315264 | bytes 19922944 | tf_op jit(solution)/shard_map/dot_general | solution.py:220
  367.3 3.8 all-to-all-start.4
  371.1 0.0 copy-done.5
  371.2 139.9 %all-to-all-done.4 = bf16[32,48,2048]{2,1,0:T(8,128)(2,1)} async-done(((bf16[32,48,2048]{2,1,0:T(8,128)(2,1)}), bf16[32,48,2048]{2,1,0:T(8,128)(2,1)}, u32[]{:S(2)}, u32[]{:S(2)}) %all-to-all-start.4) | async-done | bytes 6291488 | tf_op jit(solution)/shard_map/all_to_all | solution.py:413
  511.2 3.9 convolution_bitcast_fusion
  515.0 4.7 fusion.3
  (35 shorter events, 0.2 us)
Async XLA Ops:
  6.5 349.0 %copy-start = (bf16[1,512,2048]{2,1,0:T(8,128)(2,1)S(1)}, bf16[1,512,2048]{2,1,0:T(8,128)(2,1)}, u32[]{:S(2)}) copy-start(bf16[1,512,2048]{2,1,0:T(8,128)(2,1)} %param.37) | copy-start | bytes 6291460
  6.5 92.8 %all-gather.2.cloned.1.call-start = ((), (), s32[]{:S(2)}) async-start(), calls=%async_computation.6 | async-start | bytes 2359296 | tf_op jit(solution)/shard_map/all_gather | solution.py:261
  10.7 25.7 %all-to-all-start = ((bf16[8,6,2048]{2,1,0:T(8,128)(2,1)}), bf16[8,6,2048]{2,1,0:T(8,128)(2,1)S(1)}, u32[]{:S(2)}, u32[]{:S(2)}) async-start(bf16[8,6,2048]{2,1,0:T(8,128)(2,1)} %broadcast_in_dim.35), calls=%async_computation | async-start | bytes 524288 | tf_op jit(solution)/shard_map/all_to_all | solution.py:271
  18.0 182.4 %reduce-scatter.2.cloned.1.call-start = ((), (), s32[]{:S(2)}) async-start(), calls=%async_computation.7 | async-start | bytes 2621440 | tf_op jit(solution)/shard_map/reduce_scatter | solution.py:386
  23.4 13.1 %copy-start.8 = (s32[8]{0:T(128)}, s32[8]{0:T(128)S(1)}, u32[]{:S(2)}) copy-start(s32[8]{0:T(128)S(1)} %select_reduce_fusion.1.slot_ref) | copy-start | bytes 100
  30.0 5.0 copy-start.4
  151.6 13.4 %copy-start.9 = (bf16[1024,2048]{1,0:T(8,128)(2,1)S(1)}, bf16[1024,2048]{1,0:T(8,128)(2,1)}, u32[]{:S(2)}) copy-start(bf16[1024,2048]{1,0:T(8,128)(2,1)} %param.30) | copy-start | bytes 12582916
  165.1 5.0 copy-start.6
  170.0 30.4 %copy-start.2 = (bf16[128,2048]{1,0:T(8,128)(2,1)S(1)}, bf16[128,2048]{1,0:T(8,128)(2,1)}, u32[]{:S(2)}) copy-start(bf16[128,2048]{1,0:T(8,128)(2,1)} %param.31) | copy-start | bytes 1572868
  170.0 31.7 %copy-start.7 = (f32[2048]{0:T(1024)S(1)}, f32[2048]{0:T(1024)}, u32[]{:S(2)}) copy-start(f32[2048]{0:T(1024)} %param.32) | copy-start | bytes 24580
  204.6 145.7 %copy-start.10 = (bf16[1,2048,512]{2,1,0:T(8,128)(2,1)S(1)}, bf16[1,2048,512]{2,1,0:T(8,128)(2,1)}, u32[]{:S(2)}) copy-start(bf16[1,2048,512]{2,1,0:T(8,128)(2,1)} %param.35) | copy-start | bytes 6291460
  347.6 2.7 copy-start.1
  367.3 3.9 copy-start.5
  367.3 143.9 %all-to-all-start.4 = ((bf16[32,48,2048]{2,1,0:T(8,128)(2,1)}), bf16[32,48,2048]{2,1,0:T(8,128)(2,1)}, u32[]{:S(2)}, u32[]{:S(2)}) async-start(bf16[32,48,2048]{2,1,0:T(8,128)(2,1)} %bitcast.72), calls=%async_computation.5 | async-start | bytes 12582912 | tf_op jit(solution)/shard_map/all_to_all | solution.py:413
  511.2 3.9 copy-start.3
Sparse Core Ops, SparseCore 0:
  9.5 54.6 all-gather.1
  170.1 30.2 reduce-scatter.1

commit v3 on v2

--- a/solution.py
+++ b/solution.py
@@ -36,6 +36,17 @@
         + product(left_high, right_low, contract)
         + product(left_low, right_high, contract)
     )
+
+
+def fine_halves(left, right):
+    left_high, left_low = left
+    right_high, right_low = right
+    contract = ((1,), (0,))
+    return product(
+        jnp.concatenate([left_high, left_low], axis=1),
+        jnp.concatenate([right_high, right_high], axis=0),
+        contract,
+    ) + product(left_high, right_low, contract)
 
 
 def coarse(left, right, contract=((1,), (0,))):
@@ -59,6 +70,7 @@
     group_width = (2 + GROUP) * HEAD
     heads = row_ref.shape[2] // BLOCK
     cols = row_ref[0].T
+    lowers, sides = [], []
     for pack in range(heads // PACK):
         queries, keys, values = [], [], []
         for group in range(PACK // GROUP):
@@ -89,22 +101,28 @@
         across = ((1,), (1,))
         lower = jnp.where(strict, beta * fine(key, key, across) * decay, 0.0)
         mix_ref[0, rows, :] = (coarse(query, key, across) * decay).astype(jnp.bfloat16)
-        inverse = jnp.where(row_id == col_id, 1.0, 0.0) - jnp.where(
-            row_id // 2 == col_id // 2, lower, 0.0
-        )
-        size = 2
-        while size < BLOCK:
-            joint = (row_id // (2 * size) == col_id // (2 * size)) & (row_id // size != col_id // size)
-            between = jnp.where(joint, lower, 0.0)
-            inverse = inverse - fine(fine(inverse, between), inverse)
-            size *= 2
-        solved = fine(
-            inverse, jnp.concatenate([(beta * growth) * key, beta * value], axis=1)
-        )
         query_ref[0, rows, :] = (growth * query).astype(jnp.bfloat16)
         key_ref[0, rows, :] = tail * key
-        weighted_ref[0, rows, :] = solved[:, :HEAD]
-        values_ref[0, rows, :] = solved[:, HEAD:]
+        lowers.append(lower)
+        sides.append(jnp.concatenate([(beta * growth) * key, beta * value], axis=1))
+    unit = jnp.where(row_id == col_id, 1.0, 0.0)
+    pairs = row_id // 2 == col_id // 2
+    inverses = [unit - jnp.where(pairs, lower, 0.0) for lower in lowers]
+    size = 2
+    while size < BLOCK:
+        joint = (row_id // (2 * size) == col_id // (2 * size)) & (row_id // size != col_id // size)
+        halves = [split(inverse) for inverse in inverses]
+        between = [split(jnp.where(joint, lower, 0.0)) for lower in lowers]
+        steps = [fine_halves(half, mid) for half, mid in zip(halves, between)]
+        steps = [split(step) for step in steps]
+        steps = [fine_halves(step, half) for step, half in zip(steps, halves)]
+        inverses = [inverse - step for inverse, step in zip(inverses, steps)]
+        size *= 2
+    solved = [fine_halves(split(inverse), split(side)) for inverse, side in zip(inverses, sides)]
+    for pack, one in enumerate(solved):
+        rows = slice(pack * LANES, (pack + 1) * LANES)
+        weighted_ref[0, rows, :] = one[:, :HEAD]
+        values_ref[0, rows, :] = one[:, HEAD:]
 
 
 def maps_kernel(first_ref, slot_ref, key_ref, weighted_ref, values_ref, col_ref, cache_ref, out_ref, total):
@@ -129,15 +147,22 @@
                 [jnp.zeros((HEAD, HEAD), jnp.float32), cache_ref[0, head].astype(jnp.float32)], axis=1
             )
 
+    spans = [slice(head * BLOCK, (head + 1) * BLOCK) for head in range(heads)]
+    states = [total[head] for head in range(heads)]
+    blank = jnp.zeros((BLOCK, HEAD), jnp.float32)
+    moved = [
+        fine_halves(split(weighted_ref[0, rows, :]), split(state)) for rows, state in zip(spans, states)
+    ]
+    fixed = [
+        jnp.concatenate([blank, values_ref[0, rows, :]], axis=1) - move
+        for rows, move in zip(spans, moved)
+    ]
+    added = [
+        fine(key_ref[0, rows, :], part, ((0,), (0,))) for rows, part in zip(spans, fixed)
+    ]
     for head in range(heads):
-        rows = slice(head * BLOCK, (head + 1) * BLOCK)
-        state = total[head]
-        fixed = (
-            jnp.concatenate([jnp.zeros((BLOCK, HEAD), jnp.float32), values_ref[0, rows, :]], axis=1)
-            - fine(weighted_ref[0, rows, :], state)
-        )
         last = col_ref[0, 4:5, head * BLOCK : head * BLOCK + 1]
-        total[head] = last * state + fine(key_ref[0, rows, :], fixed, ((0,), (0,)))
+        total[head] = last * states[head] + added[head]
 
     @pl.when(block == pl.num_programs(0) - 1)
     def _():
@@ -190,20 +215,28 @@
         for head in range(heads):
             total[head] = cache_ref[0, head].astype(jnp.float32)
 
+    spans = [slice(head * BLOCK, (head + 1) * BLOCK) for head in range(heads)]
+    states = [total[head] for head in range(heads)]
+    halves = [split(state) for state in states]
+    moved = [
+        fine_halves(split(weighted_ref[0, rows, :]), half) for rows, half in zip(spans, halves)
+    ]
+    outputs = [
+        product(query_ref[0, rows, :], half[0], ((1,), (0,))) for rows, half in zip(spans, halves)
+    ]
+    fixed = [values_ref[0, rows, :] - move for rows, move in zip(spans, moved)]
+    added = [
+        fine(key_ref[0, rows, :], part, ((0,), (0,))) for rows, part in zip(spans, fixed)
+    ]
+    for head in range(heads):
+        last = col_ref[0, 4:5, head * BLOCK : head * BLOCK + 1]
+        total[head] = last * states[head] + added[head]
+    fixed = [part.astype(jnp.bfloat16) for part in fixed]
     for pack in range(heads // PACK):
-        fixed_rows, outputs = [], []
-        for inner in range(PACK):
-            head = pack * PACK + inner
-            rows = slice(head * BLOCK, (head + 1) * BLOCK)
-            state = total[head]
-            fixed = values_ref[0, rows, :] - fine(weighted_ref[0, rows, :], state)
-            outputs.append(product(query_ref[0, rows, :], state.astype(jnp.bfloat16), ((1,), (0,))))
-            last = col_ref[0, 4:5, head * BLOCK : head * BLOCK + 1]
-            total[head] = last * state + fine(key_ref[0, rows, :], fixed, ((0,), (0,)))
-            fixed_rows.append(fixed.astype(jnp.bfloat16))
         rows = slice(pack * LANES, (pack + 1) * LANES)
-        core = jnp.concatenate(outputs, axis=0) + product(
-            mix_ref[0, rows, :], jnp.concatenate(fixed_rows, axis=0), ((1,), (0,))
+        members = slice(pack * PACK, (pack + 1) * PACK)
+        core = jnp.concatenate(outputs[members], axis=0) + product(
+            mix_ref[0, rows, :], jnp.concatenate(fixed[members], axis=0), ((1,), (0,))
         )
         core = core * lax.rsqrt(jnp.mean(core * core, axis=1, keepdims=True) + 1e-06) * gain_ref[...]
         for inner in range(PACK):

time: 528 us -> 486 us (0.920)
  Pallas kernels: 94.5 us -> 52 us
    pallas_call x1, Pallas kernels: 61 us -> 24.5 us  [local(): pl.pallas_call(parts_kernel, grid=(blocks,), in_specs=[pl.BlockSpec((BLOC...]
  transfers between devices with their start and end apart: 4 -> 4, of which waited for: 2 -> 3; matrix products, arithmetic and copies ran while one was open for 4% -> 5% of each run, Pallas kernels for 12% -> 5%
where the time goes in v3:
time: 486 us; the launch traced here: 484 us
  blocking collectives  174 us (36%)
  waiting for transfers between devices  171 us (35%)
  Pallas kernels  52 us (11%)
  matrix products  33.3 us (7%)
  local copies, waits for them, and re-layouts  17.3 us (4%)
  between operations  13.6 us (3%)
  other arithmetic  11.8 us (2%)
  starting transfers between devices  11.2 us (2%)
    all_to_all x1, blocking collectives, local(): lax.all_to_all(outgoing, devices, split_axis=0, concat_axis=0, tiled=True)  143 us
    all_to_all x1, waiting for transfers between devices, local(): lax.all_to_all(results, devices, split_axis=0, concat_axis=0, tiled=True)  140 us
    reduce_scatter x1, waiting for transfers between devices, local(): lax.psum_scatter(jnp.dot(rows_in, out_weight, preferred_element_type=jnp....  29.6 us
    pallas_call x1, Pallas kernels, local(): pl.pallas_call(parts_kernel, grid=(blocks,), in_specs=[pl.BlockSpec((BLOC...  24.5 us
    all_to_all x1, blocking collectives, local(): swapped = lax.all_to_all(own_map, 'seq', 0, 0, tiled=True)  18.6 us
    all_to_all x1, blocking collectives, local(): lax.all_to_all(enter_states(swapped.reshape(seq_count, -1, HEAD, 2 * HEAD...  12.3 us
    dot_general x1, matrix products, expert_apply(): jnp.dot(hidden, expert_down[0], preferred_element_type=jnp.float32)  11.8 us
    pallas_call x1, Pallas kernels, local(): pl.pallas_call(advance_kernel, grid_spec=pltpu.PrefetchScalarGridSpec(num...  11.5 us
  transfers between devices with their start and end apart: 4, of which 3 were waited for; matrix products, arithmetic and copies ran while one was open for 5% of the time, Pallas kernels for 5%

profile of v3, /device:TPU:0, one launch (start us, length us, event | category | flops | bytes accessed | tf_op | source)
XLA Modules:
  0.0 484.0 jit_solution(3014676539092166428)
XLA Ops:
  6.5 0.0 copy-start
  6.5 1.9 convert_element_type.79
  8.5 0.0 all-gather.2.cloned.1.call-update
  8.5 0.7 convert_bitcast_fusion
  9.3 0.7 slice_bitcast_fusion
  10.0 0.7 broadcast_in_dim.35
  10.7 7.3 %all-to-all-start = ((bf16[8,6,2048]{2,1,0:T(8,128)(2,1)}), bf16[8,6,2048]{2,1,0:T(8,128)(2,1)S(1)}, u32[]{:S(2)}, u32[]{:S(2)}) async-start(bf16[8,6,2048]{2,1,0:T(8,128)(2,1)} %broadcast_in_dim.35), calls=%async_computation | async-start | bytes 524288 | tf_op jit(solution)/shard_map/all_to_all | solution.py:304
  18.0 0.0 reduce-scatter.2.cloned.1.call-start
  18.1 0.7 neg.15
  18.7 0.8 fusion.31
  19.5 0.1 reshape.145
  19.6 1.8 reduce_window_sum.22
  21.4 0.1 stack.11
  21.5 0.2 exponential_reduce_fusion
  21.6 0.1 sub.36
  21.7 0.1 sub.37
  21.8 0.7 dynamic_slice.11
  22.5 0.8 select_reduce_fusion.1.slot_ref
  23.4 0.8 add_compare_fusion
  24.2 0.7 add_divide_fusion
  24.9 0.6 fusion.36
  25.5 4.5 reshape_reshape.3
  30.0 1.0 slice.32
  31.0 0.1 stack_broadcast_in_dim.7
  31.1 0.1 stack_broadcast_in_dim.8
  31.2 0.1 reshape.146
  31.3 0.1 stack.12
  31.4 3.6 copy.42
  35.0 0.6 copy.45
  35.6 0.8 stack.13.row_ref.col_ref
  36.4 0.0 all-to-all-done
  36.5 0.1 fusion.37
  36.6 0.7 gather_fusion
  37.3 0.1 maximum_select_fusion
  37.4 0.9 pad_convert_fusion.before_ref
  38.3 24.5 %shard_map.181 = (bf16[8,512,128]{2,1,0:T(8,128)(2,1)}, f32[8,512,128]{2,1,0:T(8,128)}, f32[8,512,128]{2,1,0:T(8,128)}, f32[8,512,128]{2,1,0:T(8,128)}, bf16[8,512,128]{2,1,0:T(8,128)(2,1)}) custom-call(bf16[512,2048]{1,0:T(8,128)(2,1)} %bitcast.75, f32[8,8,2048]{2,1,0:T(8,128)} %pad_convert_fusion.before_ref, f32[4,2048]{1,0:T(4,128)} %bitcast.87, ...), custom_call_target="tpu_custom_call" | custom-call | flops 5368709120 | bytes 16777216 | tf_op jit(solution)/shard_map/pallas_call | solution.py:341
  62.8 1.3 all-gather.2.cloned.1.call-done.cache_ref
  64.1 10.9 %shard_map.182 = bf16[8,128,256]{2,1,0:T(8,128)(2,1)} custom-call(s32[8]{0:T(128)} %get-tuple-element.19.first_ref, s32[8]{0:T(128)} %copy-done.8, f32[8,512,128]{2,1,0:T(8,128)} %get-tuple-element.10.key_ref, f32[8,512,128]{2,1,0:T(8,128)} %get-tuple-element.11.weighted_ref, f32[8,512,128]{2,1,0:T(8,128)} %get-tuple-element.12.values_ref, ...), custom_call_target="tpu_custom_call" | custom-call | tf_op jit(solution)/shard_map/pallas_call | solution.py:365
  75.0 18.6 %all_to_all.36 = bf16[8,128,256]{2,1,0:T(8,128)(2,1)} all-to-all(bf16[8,128,256]{2,1,0:T(8,128)(2,1)} %shard_map.182), channel_id=1, replica_groups=mesh['seq'=8,'exp'=4] {'seq'}, dimensions={0} | all-to-all | bytes 1048576 | tf_op jit(solution)/shard_map/all_to_all | solution.py:378
  93.6 5.0 %shard_map.183 = bf16[8,1,128,128]{3,2,1,0:T(8,128)(2,1)} custom-call(bf16[8,1,128,256]{3,2,1,0:T(8,128)(2,1)} %bitcast.76), custom_call_target="tpu_custom_call" | custom-call | tf_op jit(solution)/shard_map/pallas_call | solution.py:191
  98.6 12.3 %all_to_all.37.maps_ref = bf16[8,128,128]{2,1,0:T(8,128)(2,1)} all-to-all(bf16[8,128,128]{2,1,0:T(8,128)(2,1)} %bitcast.77), channel_id=1, replica_groups=mesh['seq'=8,'exp'=4] {'seq'}, dimensions={0} | all-to-all | bytes 524288 | tf_op jit(solution)/shard_map/all_to_all | solution.py:379
  110.9 11.5 %shard_map.184 = bf16[512,1024]{1,0:T(8,128)(2,1)} custom-call(s32[8]{0:T(128)} %get-tuple-element.19.first_ref, s32[8]{0:T(128)} %copy-done.8, bf16[8,128,128]{2,1,0:T(8,128)(2,1)} %all_to_all.37.maps_ref, bf16[8,512,128]{2,1,0:T(8,128)(2,1)} %get-tuple-element.13.query_ref, f32[8,512,128]{2,1,0:T(8,128)} %get-tuple-element.10.key_ref, ...), custom_call_target="tpu_custom_call" | custom-call | tf_op jit(solution)/shard_map/pallas_call | solution.py:392
  122.4 0.0 copy-start.6
  122.4 4.9 %convolution_convert_fusion.2 = bf16[512,2048]{1,0:T(8,128)(2,1)} fusion(bf16[512,1024]{1,0:T(8,128)(2,1)} %shard_map.184, bf16[1024,2048]{1,0:T(8,128)(2,1)S(1)} %copy-done.9), kind=kOutput, calls=%fused_computation.5 | convolution fusion | flops 2148532224 | bytes 7340032 | tf_op jit(solution)/shard_map/dot_general | solution.py:420
  127.4 0.0 reduce-scatter.2.cloned.1.call-update
  127.4 0.1 copy.40
  127.5 0.2 reduce_window_sum.23
  127.7 0.1 copy.41
  127.8 0.1 eq.61
  127.9 0.3 fusion.14
  128.2 29.6 %reduce-scatter.2.cloned.1.call-done = bf16[128,2048]{1,0:T(8,128)(2,1)} async-done(((bf16[512,2048]{1,0:T(8,128)(2,1)}), bf16[128,2048]{1,0:T(8,128)(2,1)}) %reduce-scatter.2.cloned.1.call-update) | async-done | bytes 524304 | tf_op jit(solution)/shard_map/reduce_scatter | solution.py:419
  157.8 1.3 fusion.8
  159.1 0.0 copy-done.7
  159.1 2.9 convolution_convert_fusion.1
  162.0 0.0 copy-start.10
  162.0 143.0 %all_to_all.38 = bf16[32,48,2048]{2,1,0:T(8,128)(2,1)S(1)} all-to-all(bf16[32,48,2048]{2,1,0:T(8,128)(2,1)S(1)} %bitcast.70), channel_id=1, replica_groups=mesh['seq'=8,'exp'=4] {'seq','exp'}, dimensions={0} | all-to-all | bytes 12582912 | tf_op jit(solution)/shard_map/all_to_all | solution.py:444
  305.1 2.7 copy-done.1
  307.7 0.0 copy-done.10
  307.7 5.2 %fusion.6 = f32[1536,512]{1,0:T(8,128)} fusion(bf16[1536,2048]{1,0:T(8,128)(2,1)S(1)} %bitcast.73, bf16[1,2048,512]{2,1,0:T(8,128)(2,1)S(1)} %copy-done.10), kind=kOutput, calls=%fused_computation.13 | convolution fusion | flops 3221225472 | bytes 11534336 | tf_op jit(solution)/shard_map/dot_general | solution.py:250
  312.9 11.8 %convolution_convert_fusion = bf16[1536,2048]{1,0:T(8,128)(2,1)} fusion(bf16[1,512,2048]{2,1,0:T(8,128)(2,1)S(1)} %copy-done, bf16[1536,2048]{1,0:T(8,128)(2,1)} %bitcast.74, f32[1536,512]{1,0:T(8,128)} %fusion.6, bf16[1,2048,512]{2,1,0:T(8,128)(2,1)} %param.36), kind=kOutput, calls=%fused_computation.1 | convolution fusion | flops 6450315264 | bytes 19922944 | tf_op jit(solution)/shard_map/dot_general | solution.py:253
  324.7 3.9 all-to-all-start.4
  328.6 139.9 %all-to-all-done.4 = bf16[32,48,2048]{2,1,0:T(8,128)(2,1)} async-done(((bf16[32,48,2048]{2,1,0:T(8,128)(2,1)}), bf16[32,48,2048]{2,1,0:T(8,128)(2,1)}, u32[]{:S(2)}, u32[]{:S(2)}) %all-to-all-start.4) | async-done | bytes 6291488 | tf_op jit(solution)/shard_map/all_to_all | solution.py:446
  468.6 3.9 convolution_bitcast_fusion
  472.5 4.7 fusion.3
  (35 shorter events, 0.2 us)
Async XLA Ops:
  6.5 306.4 %copy-start = (bf16[1,512,2048]{2,1,0:T(8,128)(2,1)S(1)}, bf16[1,512,2048]{2,1,0:T(8,128)(2,1)}, u32[]{:S(2)}) copy-start(bf16[1,512,2048]{2,1,0:T(8,128)(2,1)} %param.37) | copy-start | bytes 6291460
  6.5 57.6 %all-gather.2.cloned.1.call-start = ((), (), s32[]{:S(2)}) async-start(), calls=%async_computation.6 | async-start | bytes 2359296 | tf_op jit(solution)/shard_map/all_gather | solution.py:294
  10.7 25.7 %all-to-all-start = ((bf16[8,6,2048]{2,1,0:T(8,128)(2,1)}), bf16[8,6,2048]{2,1,0:T(8,128)(2,1)S(1)}, u32[]{:S(2)}, u32[]{:S(2)}) async-start(bf16[8,6,2048]{2,1,0:T(8,128)(2,1)} %broadcast_in_dim.35), calls=%async_computation | async-start | bytes 524288 | tf_op jit(solution)/shard_map/all_to_all | solution.py:304
  18.0 139.8 %reduce-scatter.2.cloned.1.call-start = ((), (), s32[]{:S(2)}) async-start(), calls=%async_computation.7 | async-start | bytes 2621440 | tf_op jit(solution)/shard_map/reduce_scatter | solution.py:419
  23.4 13.1 %copy-start.8 = (s32[8]{0:T(128)}, s32[8]{0:T(128)S(1)}, u32[]{:S(2)}) copy-start(s32[8]{0:T(128)S(1)} %select_reduce_fusion.1.slot_ref) | copy-start | bytes 100
  30.0 5.0 %copy-start.4 = (f32[4,4,512]{2,1,0:T(4,128)S(1)}, f32[4,4,512]{2,1,0:T(4,128)}, u32[]{:S(2)}) copy-start(f32[4,4,512]{2,1,0:T(4,128)} %param.24) | copy-start | bytes 98308
  110.9 11.5 %copy-start.9 = (bf16[1024,2048]{1,0:T(8,128)(2,1)S(1)}, bf16[1024,2048]{1,0:T(8,128)(2,1)}, u32[]{:S(2)}) copy-start(bf16[1024,2048]{1,0:T(8,128)(2,1)} %param.30) | copy-start | bytes 12582916
  122.4 5.0 %copy-start.6 = (s32[128,10]{0,1:T(8,128)S(1)}, s32[128,10]{0,1:T(8,128)}, u32[]{:S(2)}) copy-start(s32[128,10]{0,1:T(8,128)} %param.33) | copy-start | bytes 15364
  127.4 30.4 %copy-start.2 = (bf16[128,2048]{1,0:T(8,128)(2,1)S(1)}, bf16[128,2048]{1,0:T(8,128)(2,1)}, u32[]{:S(2)}) copy-start(bf16[128,2048]{1,0:T(8,128)(2,1)} %param.31) | copy-start | bytes 1572868
  127.4 31.7 %copy-start.7 = (f32[2048]{0:T(1024)S(1)}, f32[2048]{0:T(1024)}, u32[]{:S(2)}) copy-start(f32[2048]{0:T(1024)} %param.32) | copy-start | bytes 24580
  162.0 145.7 %copy-start.10 = (bf16[1,2048,512]{2,1,0:T(8,128)(2,1)S(1)}, bf16[1,2048,512]{2,1,0:T(8,128)(2,1)}, u32[]{:S(2)}) copy-start(bf16[1,2048,512]{2,1,0:T(8,128)(2,1)} %param.35) | copy-start | bytes 6291460
  305.0 2.7 copy-start.1
  324.7 3.9 copy-start.5
  324.7 143.9 %all-to-all-start.4 = ((bf16[32,48,2048]{2,1,0:T(8,128)(2,1)}), bf16[32,48,2048]{2,1,0:T(8,128)(2,1)}, u32[]{:S(2)}, u32[]{:S(2)}) async-start(bf16[32,48,2048]{2,1,0:T(8,128)(2,1)} %bitcast.72), calls=%async_computation.5 | async-start | bytes 12582912 | tf_op jit(solution)/shard_map/all_to_all | solution.py:446
  468.6 3.9 copy-start.3
Sparse Core Ops, SparseCore 0:
  9.5 54.5 all-gather.1
  127.5 30.2 reduce-scatter.1
